TPU v7x, 32 devices: a whole 2x2x4 slice. The times are simulated.
32 devices in a mesh: dp: 8 (over z, core), cp: 4 (over y, x).
Axes of the slice: x: 2, y: 2, z: 4, core: 2. Of those that a mesh axis runs over, the one named last changes fastest.
Arguments:
- tokens: bfloat16 [8, 2, 3072, 1088], P('dp', None, 'cp'), may hold values from -6 to 6
- cotangent: bfloat16 [8, 2, 3072, 1088], P('dp', None, 'cp'), may hold values from -6 to 6
- seq_lengths: int32 [8, 2, 3], P('dp'), may hold values from 1 to 2048, as said below
- block_order: int32 [8, 2, 4], P('dp'), may hold values from 0 to 3, as said below
- norm_gain: bfloat16 [2, 1088], P(None, 'dp'), may hold values from 0.5 to 1.5
- norm_shift: bfloat16 [2, 1088], P(None, 'dp'), may hold values from -1.25 to 1.25
- mix_weight: bfloat16 [1088, 3, 1088], P('dp', None, 'cp'), may hold values from -0.1875 to 0.1875
- mix_bias: bfloat16 [2, 1088], P(None, 'dp'), may hold values from -0.625 to 0.625
- out_weight: bfloat16 [1088, 1088], P('dp', 'cp'), may hold values from -1 to 1
- up_weight: bfloat16 [1088, 4352], P('dp', 'cp'), may hold values from -0.1875 to 0.1875
- up_bias: bfloat16 [4352], P('dp'), may hold values from -1.25 to 1.25
- down_weight: bfloat16 [4352, 1088], P('dp', 'cp'), may hold values from -0.09375 to 0.09375
- out_bias: bfloat16 [2, 1088], P(None, 'dp'), may hold values from -1.25 to 1.25
Outputs:
- layer_out: bfloat16 [8, 2, 3072, 1088], P('dp', None, 'cp')
- grad_tokens: bfloat16 [8, 2, 3072, 1088], P('dp', None, 'cp')
- grad_norm_gain: float32 [2, 1088], P(None, 'dp')
- grad_norm_shift: float32 [2, 1088], P(None, 'dp')
- grad_mix_weight: float32 [1088, 3, 1088], P('dp', None, 'cp')
- grad_mix_bias: float32 [2, 1088], P(None, 'dp')
- grad_out_weight: float32 [1088, 1088], P('dp', 'cp')
- grad_up_weight: float32 [1088, 4352], P('dp', 'cp')
- grad_up_bias: float32 [4352], P('dp')
- grad_down_weight: float32 [4352, 1088], P('dp', 'cp')
- grad_out_bias: float32 [2, 1088], P(None, 'dp')
Inputs may be any that keep to these rules, and one draw needn't show every extreme that they name: `seq_lengths`: the 3 lengths of each pack, in order, fill its 3072 positions exactly; the longest sequence of every pack has 2048 tokens. For each pack, a permutation of the 4 blocks: device j along cp holds pack positions block_order[g, m, j] * 768 up to block_order[g, m, j] * 768 + 767.
All inputs are finite; a program needn't handle non-finite values.
Results may differ from a plain program's by a relative error of at most 0.019.
Values may be sent and summed in bfloat16 or wider, within the bound.
No kernel may reach another device: no remote copies, remote signals or barrier semaphores. Data moves between devices by JAX's collectives and lax.ppermute only.
A program may use at most 384 MiB of HBM per device.

v0:
```python
import jax
import jax.numpy as jnp
from jax import lax
from jax.sharding import PartitionSpec as P

HEAD_DIM = 64
FF = 4352


EPS = 1e-05
NEG = -1e30


def layer_norm(rows, gain, shift):
    center = rows - jnp.mean(rows, axis=-1, keepdims=True)
    spread = jnp.mean(center * center, axis=-1, keepdims=True)
    return center * lax.rsqrt(spread + EPS) * gain + shift


def gelu_exact(values):
    return jax.nn.gelu(values, approximate=False)


def sequence_ids(places, lengths):
    bounds = jnp.cumsum(lengths, dtype=jnp.int32)
    return jnp.sum((places[:, None] >= bounds[None, :]).astype(jnp.int32), axis=1, dtype=jnp.int32)


def key_places(start, count, order_row, lengths, rows):
    index = start + jnp.arange(count, dtype=jnp.int32)
    owner = index // rows
    slots = jnp.arange(order_row.shape[0], dtype=jnp.int32)
    block = jnp.sum(
        jnp.where(owner[:, None] == slots[None, :], order_row[None, :], 0), axis=1, dtype=jnp.int32
    )
    places = block * rows + index % rows
    return (places, sequence_ids(places, lengths))


def gather_weights(shards):
    (
        norm_gain,
        norm_shift,
        mix_weight,
        mix_bias,
        out_weight,
        up_weight,
        up_bias,
        down_weight,
        out_bias,
    ) = shards
    columns = (
        lax.all_gather(mix_weight, "cp", axis=2, tiled=True),
        lax.all_gather(out_weight, "cp", axis=1, tiled=True),
        lax.all_gather(up_weight, "cp", axis=1, tiled=True),
        lax.all_gather(down_weight, "cp", axis=1, tiled=True),
    )
    return (
        lax.all_gather(columns[0], "dp", axis=0, tiled=True),
        lax.all_gather(columns[1], "dp", axis=0, tiled=True),
        lax.all_gather(columns[2], "dp", axis=0, tiled=True),
        lax.all_gather(columns[3], "dp", axis=0, tiled=True),
        lax.all_gather(norm_gain, "dp", axis=1, tiled=True),
        lax.all_gather(norm_shift, "dp", axis=1, tiled=True),
        lax.all_gather(mix_bias, "dp", axis=1, tiled=True),
        lax.all_gather(up_bias, "dp", axis=0, tiled=True),
        lax.all_gather(out_bias, "dp", axis=1, tiled=True),
    )


def per_device(
    tokens,
    cotangent,
    seq_lengths,
    block_order,
    norm_gain,
    norm_shift,
    mix_weight,
    mix_bias,
    out_weight,
    up_weight,
    up_bias,
    down_weight,
    out_bias,
):
    shards = (
        norm_gain,
        norm_shift,
        mix_weight,
        mix_bias,
        out_weight,
        up_weight,
        up_bias,
        down_weight,
        out_bias,
    )
    micro = tokens.shape[1]
    rows = tokens.shape[2]
    width = tokens.shape[3]
    heads = width // HEAD_DIM
    scale = HEAD_DIM ** (-0.5)
    devices_cp = lax.axis_size("cp")
    device = lax.axis_index("cp")
    grad_mix = jnp.zeros((width, 3 * width), jnp.float32)
    grad_proj = jnp.zeros((width, width), jnp.float32)
    grad_up = jnp.zeros((width, FF), jnp.float32)
    grad_down = jnp.zeros((FF, width), jnp.float32)
    grad_gain = jnp.zeros((2, width), jnp.float32)
    grad_shift = jnp.zeros((2, width), jnp.float32)
    grad_mixb = jnp.zeros((2, width), jnp.float32)
    grad_upb = jnp.zeros((FF,), jnp.float32)
    grad_outb = jnp.zeros((2, width), jnp.float32)
    outputs = []
    input_grads = []
    for index in range(micro):
        full = gather_weights(shards)
        mix_full, out_full, up_full, down_full = (full[0], full[1], full[2], full[3])
        gains = full[4].astype(jnp.float32)
        shifts = full[5].astype(jnp.float32)
        mix_biases = full[6].astype(jnp.float32)
        up_biases = full[7].astype(jnp.float32)
        out_biases = full[8].astype(jnp.float32)
        source = tokens[0, index].astype(jnp.float32)
        order_row = block_order[0, index]
        lengths = seq_lengths[0, index]
        slots = jnp.arange(order_row.shape[0], dtype=jnp.int32)
        own_block = jnp.sum(jnp.where(slots == device, order_row, 0), dtype=jnp.int32)
        query_places = own_block * rows + jnp.arange(rows, dtype=jnp.int32)
        query_seq = sequence_ids(query_places, lengths)
        normed1, norm1_back = jax.vjp(layer_norm, source, gains[0], shifts[0])
        normed1_low = normed1.astype(jnp.bfloat16)
        mix_matrix = mix_full.reshape(width, 3 * width)
        mixed = jnp.dot(normed1_low, mix_matrix, preferred_element_type=jnp.float32)
        query_low = (
            (mixed[:, :width] + mix_biases[0]).astype(jnp.bfloat16).reshape(rows, heads, HEAD_DIM)
        )
        key_low = mixed[:, width : 2 * width].astype(jnp.bfloat16)
        value_low = (mixed[:, 2 * width :] + mix_biases[1]).astype(jnp.bfloat16)

        def allowed_for(start, count):
            places, seq_ids = key_places(start, count, order_row, lengths, rows)
            return (query_seq[:, None] == seq_ids[None, :]) & (
                places[None, :] <= query_places[:, None]
            )

        start_state = (
            jnp.full((rows, heads), NEG, jnp.float32),
            jnp.zeros((rows, heads), jnp.float32),
            jnp.zeros((rows, heads, HEAD_DIM), jnp.float32),
        )
        key_rows = lax.all_gather(key_low, "cp", axis=0, tiled=True)
        value_rows = lax.all_gather(value_low, "cp", axis=0, tiled=True)
        total = key_rows.shape[0]
        span = min(total, rows)

        def forward_visit(inner, carry):
            first = inner * span
            key_block = lax.dynamic_slice_in_dim(key_rows, first, span, 0).reshape(
                span, heads, HEAD_DIM
            )
            value_block = lax.dynamic_slice_in_dim(value_rows, first, span, 0).reshape(
                span, heads, HEAD_DIM
            )
            allowed = allowed_for(first, span)

            def forward_update(current):
                row_top, weight_sum, accumulated = current
                scores = (
                    jnp.einsum(
                        "qhd,khd->qhk", query_low, key_block, preferred_element_type=jnp.float32
                    )
                    * scale
                )
                scores = jnp.where(allowed[:, None, :], scores, NEG)
                new_top = jnp.maximum(row_top, jnp.max(scores, axis=-1))
                weights = jnp.where(allowed[:, None, :], jnp.exp(scores - new_top[..., None]), 0.0)
                factor = jnp.exp(row_top - new_top)
                weight_sum = weight_sum * factor + jnp.sum(weights, axis=-1)
                accumulated = accumulated * factor[..., None] + jnp.einsum(
                    "qhk,khd->qhd",
                    weights.astype(jnp.bfloat16),
                    value_block,
                    preferred_element_type=jnp.float32,
                )
                return (new_top, weight_sum, accumulated)

            return lax.cond(jnp.any(allowed), forward_update, lambda current: current, carry)

        row_top, weight_sum, accumulated = lax.fori_loop(
            0, total // span, forward_visit, start_state
        )
        attended = accumulated / weight_sum[..., None]
        log_sum = row_top + jnp.log(weight_sum)
        attended_low = attended.reshape(rows, width).astype(jnp.bfloat16)
        residual = (
            source
            + jnp.dot(attended_low, out_full, preferred_element_type=jnp.float32)
            + out_biases[0]
        )
        normed2, norm2_back = jax.vjp(layer_norm, residual, gains[1], shifts[1])
        normed2_low = normed2.astype(jnp.bfloat16)
        upper = jnp.dot(normed2_low, up_full, preferred_element_type=jnp.float32) + up_biases
        active, gelu_back = jax.vjp(gelu_exact, upper)
        active_low = active.astype(jnp.bfloat16)
        result = (
            residual
            + jnp.dot(active_low, down_full, preferred_element_type=jnp.float32)
            + out_biases[1]
        )
        outputs.append(result.astype(jnp.bfloat16))
        full = gather_weights(shards)
        mix_full, out_full, up_full, down_full = (full[0], full[1], full[2], full[3])
        mix_matrix = mix_full.reshape(width, 3 * width)
        grad_rows_out = cotangent[0, index]
        grad_down = grad_down + jnp.einsum(
            "tf,td->fd", active_low, grad_rows_out, preferred_element_type=jnp.float32
        )
        grad_outb = grad_outb.at[1].add(jnp.sum(grad_rows_out.astype(jnp.float32), axis=0))
        grad_active = jnp.einsum(
            "td,fd->tf", grad_rows_out, down_full, preferred_element_type=jnp.float32
        )
        grad_upper = gelu_back(grad_active)[0].astype(jnp.bfloat16)
        grad_up = grad_up + jnp.einsum(
            "td,tf->df", normed2_low, grad_upper, preferred_element_type=jnp.float32
        )
        grad_upb = grad_upb + jnp.sum(grad_upper.astype(jnp.float32), axis=0)
        grad_normed2 = jnp.einsum(
            "tf,df->td", grad_upper, up_full, preferred_element_type=jnp.float32
        )
        back_residual, back_gain2, back_shift2 = norm2_back(grad_normed2)
        grad_residual = grad_rows_out.astype(jnp.float32) + back_residual
        grad_branch = grad_residual.astype(jnp.bfloat16)
        grad_proj = grad_proj + jnp.einsum(
            "te,td->ed", attended_low, grad_branch, preferred_element_type=jnp.float32
        )
        grad_outb = grad_outb.at[0].add(jnp.sum(grad_branch.astype(jnp.float32), axis=0))
        grad_attended = (
            jnp.einsum("td,ed->te", grad_branch, out_full, preferred_element_type=jnp.float32)
            .astype(jnp.bfloat16)
            .reshape(rows, heads, HEAD_DIM)
        )
        delta = jnp.sum(grad_attended.astype(jnp.float32) * attended, axis=-1)
        back_state = (
            jnp.zeros((rows, heads, HEAD_DIM), jnp.float32),
            jnp.zeros((rows * devices_cp, 2, width), jnp.float32),
        )
        backward_key_rows = lax.all_gather(key_low, "cp", axis=0, tiled=True)
        backward_value_rows = lax.all_gather(value_low, "cp", axis=0, tiled=True)
        backward_total = backward_key_rows.shape[0]
        backward_span = min(backward_total, rows)

        def backward_visit(inner, carry):
            first = inner * backward_span
            key_block = lax.dynamic_slice_in_dim(
                backward_key_rows, first, backward_span, 0
            ).reshape(backward_span, heads, HEAD_DIM)
            value_block = lax.dynamic_slice_in_dim(
                backward_value_rows, first, backward_span, 0
            ).reshape(backward_span, heads, HEAD_DIM)
            allowed = allowed_for(first, backward_span)

            def backward_update(current):
                grad_query = current[0]
                scores = (
                    jnp.einsum(
                        "qhd,khd->qhk", query_low, key_block, preferred_element_type=jnp.float32
                    )
                    * scale
                )
                probs = jnp.where(allowed[:, None, :], jnp.exp(scores - log_sum[..., None]), 0.0)
                grad_probs = jnp.einsum(
                    "qhd,khd->qhk", grad_attended, value_block, preferred_element_type=jnp.float32
                )
                grad_scores = (probs * (grad_probs - delta[..., None])).astype(jnp.bfloat16)
                grad_query = (
                    grad_query
                    + jnp.einsum(
                        "qhk,khd->qhd", grad_scores, key_block, preferred_element_type=jnp.float32
                    )
                    * scale
                )
                grad_keys = current[1]
                grad_value = jnp.einsum(
                    "qhk,qhd->khd",
                    probs.astype(jnp.bfloat16),
                    grad_attended,
                    preferred_element_type=jnp.float32,
                )
                grad_key = (
                    jnp.einsum(
                        "qhk,qhd->khd", grad_scores, query_low, preferred_element_type=jnp.float32
                    )
                    * scale
                )
                fresh = jnp.stack(
                    (
                        grad_key.reshape(backward_span, width),
                        grad_value.reshape(backward_span, width),
                    ),
                    axis=1,
                )
                previous = lax.dynamic_slice_in_dim(grad_keys, first, backward_span, 0)
                grad_keys = lax.dynamic_update_slice_in_dim(grad_keys, previous + fresh, first, 0)
                return (grad_query, grad_keys)

            return lax.cond(jnp.any(allowed), backward_update, lambda current: current, carry)

        back_result = lax.fori_loop(0, backward_total // backward_span, backward_visit, back_state)
        grad_query = back_result[0]
        own_grads = lax.psum_scatter(
            back_result[1].astype(jnp.bfloat16), "cp", scatter_dimension=0, tiled=True
        ).astype(jnp.float32)
        grad_mixed = jnp.concatenate(
            (grad_query.reshape(rows, width), own_grads[:, 0], own_grads[:, 1]), axis=1
        ).astype(jnp.bfloat16)
        grad_mix = grad_mix + jnp.einsum(
            "td,te->de", normed1_low, grad_mixed, preferred_element_type=jnp.float32
        )
        mixed_sums = jnp.sum(grad_mixed.astype(jnp.float32), axis=0)
        grad_mixb = grad_mixb + jnp.stack((mixed_sums[:width], mixed_sums[2 * width :]))
        grad_normed1 = jnp.einsum(
            "te,de->td", grad_mixed, mix_matrix, preferred_element_type=jnp.float32
        )
        back_source, back_gain1, back_shift1 = norm1_back(grad_normed1)
        input_grads.append((grad_residual + back_source).astype(jnp.bfloat16))
        grad_gain = grad_gain + jnp.stack((back_gain1, back_gain2))
        grad_shift = grad_shift + jnp.stack((back_shift1, back_shift2))
    summed = (
        lax.psum_scatter(
            grad_mix.reshape(width, 3, width).astype(jnp.bfloat16),
            "dp",
            scatter_dimension=0,
            tiled=True,
        ).astype(jnp.float32),
        lax.psum_scatter(
            grad_proj.astype(jnp.bfloat16), "dp", scatter_dimension=0, tiled=True
        ).astype(jnp.float32),
        lax.psum_scatter(
            grad_up.astype(jnp.bfloat16), "dp", scatter_dimension=0, tiled=True
        ).astype(jnp.float32),
        lax.psum_scatter(
            grad_down.astype(jnp.bfloat16), "dp", scatter_dimension=0, tiled=True
        ).astype(jnp.float32),
        lax.psum_scatter(
            grad_gain.astype(jnp.bfloat16), "dp", scatter_dimension=1, tiled=True
        ).astype(jnp.float32),
        lax.psum_scatter(
            grad_shift.astype(jnp.bfloat16), "dp", scatter_dimension=1, tiled=True
        ).astype(jnp.float32),
        lax.psum_scatter(
            grad_mixb.astype(jnp.bfloat16), "dp", scatter_dimension=1, tiled=True
        ).astype(jnp.float32),
        lax.psum_scatter(
            grad_upb.astype(jnp.bfloat16), "dp", scatter_dimension=0, tiled=True
        ).astype(jnp.float32),
        lax.psum_scatter(
            grad_outb.astype(jnp.bfloat16), "dp", scatter_dimension=1, tiled=True
        ).astype(jnp.float32),
    )
    matrices = (
        lax.psum_scatter(
            summed[0].astype(jnp.bfloat16), "cp", scatter_dimension=2, tiled=True
        ).astype(jnp.float32),
        lax.psum_scatter(
            summed[1].astype(jnp.bfloat16), "cp", scatter_dimension=1, tiled=True
        ).astype(jnp.float32),
        lax.psum_scatter(
            summed[2].astype(jnp.bfloat16), "cp", scatter_dimension=1, tiled=True
        ).astype(jnp.float32),
        lax.psum_scatter(
            summed[3].astype(jnp.bfloat16), "cp", scatter_dimension=1, tiled=True
        ).astype(jnp.float32),
    )
    vectors = lax.psum((summed[4], summed[5], summed[6], summed[7], summed[8]), "cp")
    layer_out = jnp.stack(outputs)[None]
    grad_tokens = jnp.stack(input_grads)[None]
    return (
        layer_out,
        grad_tokens,
        vectors[0],
        vectors[1],
        matrices[0],
        vectors[2],
        matrices[1],
        matrices[2],
        vectors[3],
        matrices[3],
        vectors[4],
    )


def solution(mesh):
    placed = (
        P("dp", None, "cp", None),
        P("dp", None, "cp", None),
        P("dp", None, None),
        P("dp", None, None),
        P(None, "dp"),
        P(None, "dp"),
        P("dp", None, "cp"),
        P(None, "dp"),
        P("dp", "cp"),
        P("dp", "cp"),
        P("dp"),
        P("dp", "cp"),
        P(None, "dp"),
    )
    return jax.shard_map(
        per_device,
        mesh=mesh,
        in_specs=placed,
        out_specs=(
            P("dp", None, "cp", None),
            P("dp", None, "cp", None),
            P(None, "dp"),
            P(None, "dp"),
            P("dp", None, "cp"),
            P(None, "dp"),
            P("dp", "cp"),
            P("dp", "cp"),
            P("dp"),
            P("dp", "cp"),
            P(None, "dp"),
        ),
        check_vma=False,
    )
```

profile of v0, /device:TPU:0, one launch (start us, length us, event | category | flops | bytes accessed | tf_op | source)
XLA Modules:
  0.0 2635.0 jit_solution(17510434618728271082)
XLA Ops:
  9.3 30.5 %all_gather.36 = bf16[136,3,1088]{0,1,2:T(4,128)(2,1)} all-gather(bf16[136,3,272]{0,1,2:T(4,128)(2,1)} %copy.127), channel_id=1, replica_groups=mesh['dp'=8,'cp'=4] {'cp'}, dimensions={2}, use_global_device_ids=true | all-gather | bytes 1109760 | tf_op jit(solution)/shard_map/all_gather | solution.py:53
  79.7 40.1 %all-gather.17.cloned.1.call-done = bf16[1088,3,1088]{2,0,1:T(8,128)(2,1)} async-done(((bf16[136,3,1088]{2,0,1:T(8,128)(2,1)}), bf16[1088,3,1088]{2,0,1:T(8,128)(2,1)}) %all-gather.17.cloned.1.call-update) | async-done | bytes 7102480 | tf_op jit(solution)/shard_map/all_gather | solution.py:59
  194.3 26.1 all-reduce
  225.5 32.0 %all-gather.21.cloned.1.call-done = bf16[3072,1088]{0,1:T(8,128)(2,1)} async-done(((bf16[768,1088]{0,1:T(8,128)(2,1)}), bf16[3072,1088]{0,1:T(8,128)(2,1)}) %all-gather.21.cloned.1.call-update) | async-done | bytes 6684688 | tf_op jit(solution)/shard_map/all_gather | solution.py:152
  257.5 75.2 %all-gather.19.cloned.1.call-done = bf16[3072,1088]{0,1:T(8,128)(2,1)} async-done(((bf16[768,1088]{0,1:T(8,128)(2,1)}), bf16[3072,1088]{0,1:T(8,128)(2,1)}) %all-gather.19.cloned.1.call-update) | async-done | bytes 6684688 | tf_op jit(solution)/shard_map/all_gather | solution.py:151
  334.8 126.5 %while.80 = (s32[]{:T(128)}, f32[768,17]{0,1:T(8,128)S(1)}, f32[768,17]{0,1:T(8,128)S(1)}, f32[768,17,64]{0,2,1:T(8,128)}, s32[768]{0:T(1024)S(1)}, /*index=5*/s...) while((s32[]{:T(128)}, f32[768,17]{0,1:T(8,128)S(1)}, ...), condition=%wide.region_14.15_spmd.clone, body=%wide.region_6.14_spmd.clone.sunk | while | flops 2701350912 | bytes 141939024 | solution.py:189
  336.9 59.7 %conditional.12 = ((f32[768,17]{0,1:T(8,128)S(1)}, f32[768,17]{0,1:T(8,128)S(1)}, f32[768,17,64]{0,2,1:T(8,128)})) conditional(s32[]{:T(128)} %convert_element_type.656, (f32[768,17]{0,1:T(8,128)S(1)}, f32[768,17]{0,1:T(8,128)S(1)}, f32[768,17,64]{0,2,1:T(8,128)}) %tuple.331, (pred[768,768]{0,1:T(8,128)(4,1)S(1)}, s32[]{:T(128)}, ...), branch_computations={%region_10.10_spmd, %region_11.13_spmd} | conditional | flops 2698962432 | bytes 141312064 | solution.py:187
  374.4 22.3 bitcast_add_fusion
  401.1 57.8 %conditional.12 = ((f32[768,17]{0,1:T(8,128)S(1)}, f32[768,17]{0,1:T(8,128)S(1)}, f32[768,17,64]{0,2,1:T(8,128)})) conditional(s32[]{:T(128)} %convert_element_type.656, (f32[768,17]{0,1:T(8,128)S(1)}, f32[768,17]{0,1:T(8,128)S(1)}, f32[768,17,64]{0,2,1:T(8,128)}) %tuple.331, (pred[768,768]{0,1:T(8,128)(4,1)S(1)}, s32[]{:T(128)}, ...), branch_computations={%region_10.10_spmd, %region_11.13_spmd} | conditional | flops 2698962432 | bytes 141312064 | solution.py:187
  438.1 20.8 bitcast_add_fusion
  473.6 44.9 %all-gather.31.cloned.1.call-done = bf16[3072,1088]{0,1:T(8,128)(2,1)} async-done(((bf16[768,1088]{0,1:T(8,128)(2,1)}), bf16[3072,1088]{0,1:T(8,128)(2,1)}) %all-gather.31.cloned.1.call-update) | async-done | bytes 6684688 | tf_op jit(solution)/shard_map/all_gather | solution.py:151
  520.6 241.9 %while.81 = (s32[]{:T(128)}, f32[768,17]{0,1:T(8,128)S(1)}, f32[768,17]{0,1:T(8,128)S(1)}, f32[768,17,64]{0,2,1:T(8,128)}, s32[768]{0:T(1024)S(1)}, /*index=5*/s...) while((s32[]{:T(128)}, f32[768,17]{0,1:T(8,128)S(1)}, ...), condition=%wide.region_31.32_spmd.clone, body=%wide.region_23.31_spmd.clone.sunk | while | flops 2701350912 | bytes 141939024 | solution.py:189
  522.8 58.5 %conditional.13 = ((f32[768,17]{0,1:T(8,128)S(1)}, f32[768,17]{0,1:T(8,128)S(1)}, f32[768,17,64]{0,2,1:T(8,128)})) conditional(s32[]{:T(128)} %convert_element_type.658, (f32[768,17]{0,1:T(8,128)S(1)}, f32[768,17]{0,1:T(8,128)S(1)}, f32[768,17,64]{0,2,1:T(8,128)}) %tuple.336, (pred[768,768]{0,1:T(8,128)(4,1)S(1)}, s32[]{:T(128)}, ...), branch_computations={%region_27.27_spmd, %region_28.30_spmd} | conditional | flops 2698962432 | bytes 141312064 | solution.py:187
  560.4 20.9 bitcast_add_fusion.1
  583.5 58.5 %conditional.13 = ((f32[768,17]{0,1:T(8,128)S(1)}, f32[768,17]{0,1:T(8,128)S(1)}, f32[768,17,64]{0,2,1:T(8,128)})) conditional(s32[]{:T(128)} %convert_element_type.658, (f32[768,17]{0,1:T(8,128)S(1)}, f32[768,17]{0,1:T(8,128)S(1)}, f32[768,17,64]{0,2,1:T(8,128)}) %tuple.336, (pred[768,768]{0,1:T(8,128)(4,1)S(1)}, s32[]{:T(128)}, ...), branch_computations={%region_27.27_spmd, %region_28.30_spmd} | conditional | flops 2698962432 | bytes 141312064 | solution.py:187
  621.1 20.9 bitcast_add_fusion.1
  644.3 58.2 %conditional.13 = ((f32[768,17]{0,1:T(8,128)S(1)}, f32[768,17]{0,1:T(8,128)S(1)}, f32[768,17,64]{0,2,1:T(8,128)})) conditional(s32[]{:T(128)} %convert_element_type.658, (f32[768,17]{0,1:T(8,128)S(1)}, f32[768,17]{0,1:T(8,128)S(1)}, f32[768,17,64]{0,2,1:T(8,128)}) %tuple.336, (pred[768,768]{0,1:T(8,128)(4,1)S(1)}, s32[]{:T(128)}, ...), branch_computations={%region_27.27_spmd, %region_28.30_spmd} | conditional | flops 2698962432 | bytes 141312064 | solution.py:187
  681.8 20.7 bitcast_add_fusion.1
  704.7 57.4 %conditional.13 = ((f32[768,17]{0,1:T(8,128)S(1)}, f32[768,17]{0,1:T(8,128)S(1)}, f32[768,17,64]{0,2,1:T(8,128)})) conditional(s32[]{:T(128)} %convert_element_type.658, (f32[768,17]{0,1:T(8,128)S(1)}, f32[768,17]{0,1:T(8,128)S(1)}, f32[768,17,64]{0,2,1:T(8,128)}) %tuple.336, (pred[768,768]{0,1:T(8,128)(4,1)S(1)}, s32[]{:T(128)}, ...), branch_computations={%region_27.27_spmd, %region_28.30_spmd} | conditional | flops 2698962432 | bytes 141312064 | solution.py:187
  741.6 20.5 bitcast_add_fusion.1
  787.6 75.1 %multiply_convert_fusion.1 = (bf16[768,4352]{1,0:T(8,128)(2,1)}, f32[768,4352]{1,0:T(8,128)}, bf16[768,4352]{1,0:T(8,128)(2,1)}, f32[768,4352]{1,0:T(8,128)}, f32[768,4352]{1,0:T(8,128)}) fusion(f32[4352]{0:T(1024)S(1)} %copy-done.112, f32[768,4352]{1,0:T(8,128)} %fusion.207, bf16[1088,4352]{1,0:T(8,128)(2,1)S(1)} %copy-done.132, ...), kind=kOutput, calls=%fused_computation.155 | convolution fusion | flops 7714111488 | bytes 78005248 | tf_op jit(solution)/shard_map/dot_general | solution.py:202
  862.7 20.6 convert_reduce_fusion.4
  896.7 21.8 convert_reduce_fusion.5
  1010.6 47.4 %reduce-scatter.36.cloned.1.call-done = bf16[136,1088]{1,0:T(8,128)(2,1)} async-done(((bf16[1088,1088]{1,0:T(8,128)(2,1)}), bf16[136,1088]{1,0:T(8,128)(2,1)}) %reduce-scatter.36.cloned.1.call-update) | async-done | bytes 295952
  1060.1 104.0 %reduce-scatter.28.cloned.1.call-done = bf16[544,1088]{1,0:T(8,128)(2,1)} async-done(((bf16[4352,1088]{1,0:T(8,128)(2,1)}), bf16[544,1088]{1,0:T(8,128)(2,1)}) %reduce-scatter.28.cloned.1.call-update) | async-done | bytes 1183760 | tf_op jit(solution)/shard_map/reduce_scatter | solution.py:341
  1170.2 94.7 %reduce-scatter.26.cloned.1.call-done = bf16[136,4352]{1,0:T(8,128)(2,1)} async-done(((bf16[1088,4352]{1,0:T(8,128)(2,1)}), bf16[136,4352]{1,0:T(8,128)(2,1)}) %reduce-scatter.26.cloned.1.call-update) | async-done | bytes 1183760 | tf_op jit(solution)/shard_map/reduce_scatter | solution.py:338
  1283.3 387.1 %while.83 = (s32[]{:T(128)}, f32[768,17,64]{0,2,1:T(8,128)}, f32[3072,2,1088]{0,2,1:T(8,128)}, s32[768]{0:T(1024)S(1)}, s32[1,1,4]{2,1,0:T(1,128)S(1)}, /*index=...) while((s32[]{:T(128)}, f32[768,17,64]{0,2,1:T(8,128)}, ...), condition=%wide.region_56.57_spmd.clone, body=%wide.region_50.56_spmd.clone.sunk | while | flops 6525792768 | bytes 270038496 | solution.py:308
  1286.6 94.4 %conditional.15 = ((f32[768,17,64]{0,2,1:T(8,128)}, f32[3072,2,1088]{0,2,1:T(8,128)})) conditional(s32[]{:T(128)} %convert_element_type.662, (f32[768,17,64]{0,2,1:T(8,128)}, f32[3072,2,1088]{0,2,1:T(8,128)}) %tuple.346, (pred[768,768]{0,1:T(8,128)(4,1)}, s32[]{:T(128)}, bf16[3072,1088]{0,1:T(8,128)(2,1)}, bf16[768,17,64]{0,2,1:T(8,128)(2,1)S(1)}, ...), branch_computations={%region_54.54_spmd, %region_55.55_spmd} | conditional | flops 6523404288 | bytes 269411520 | solution.py:306
  1306.3 26.7 %fusion.42 = bf16[768,17,768]{0,2,1:T(8,128)(2,1)} fusion(f32[17,768,768]{2,1,0:T(8,128)} %fusion.225, f32[768,17]{0,1:T(8,128)S(1)} %get-tuple-element.1702, f32[768,17]{0,1:T(8,128)S(1)} %get-tuple-element.1699, pred[768,768]{0,1:T(8,128)(4,1)} %get-tuple-element.1695, bf16[768,17,64]{0,2,1:T(8,128)(2,1)} %bitcast.391, ...), kind=kOutput, calls=%fused_computation.53 | convolution fusion | flops 1343619072 | bytes 64198656 | tf_op jit(solution)/shard_map/while/body/eval_jaxpr/cond/branch_1_fun/qhd,khd->qhk/dot_general | solution.py:271
  1384.0 93.4 %conditional.15 = ((f32[768,17,64]{0,2,1:T(8,128)}, f32[3072,2,1088]{0,2,1:T(8,128)})) conditional(s32[]{:T(128)} %convert_element_type.662, (f32[768,17,64]{0,2,1:T(8,128)}, f32[3072,2,1088]{0,2,1:T(8,128)}) %tuple.346, (pred[768,768]{0,1:T(8,128)(4,1)}, s32[]{:T(128)}, bf16[3072,1088]{0,1:T(8,128)(2,1)}, bf16[768,17,64]{0,2,1:T(8,128)(2,1)S(1)}, ...), branch_computations={%region_54.54_spmd, %region_55.55_spmd} | conditional | flops 6523404288 | bytes 269411520 | solution.py:306
  1403.1 26.5 %fusion.42 = bf16[768,17,768]{0,2,1:T(8,128)(2,1)} fusion(f32[17,768,768]{2,1,0:T(8,128)} %fusion.225, f32[768,17]{0,1:T(8,128)S(1)} %get-tuple-element.1702, f32[768,17]{0,1:T(8,128)S(1)} %get-tuple-element.1699, pred[768,768]{0,1:T(8,128)(4,1)} %get-tuple-element.1695, bf16[768,17,64]{0,2,1:T(8,128)(2,1)} %bitcast.391, ...), kind=kOutput, calls=%fused_computation.53 | convolution fusion | flops 1343619072 | bytes 64198656 | tf_op jit(solution)/shard_map/while/body/eval_jaxpr/cond/branch_1_fun/qhd,khd->qhk/dot_general | solution.py:271
  1480.4 93.6 %conditional.15 = ((f32[768,17,64]{0,2,1:T(8,128)}, f32[3072,2,1088]{0,2,1:T(8,128)})) conditional(s32[]{:T(128)} %convert_element_type.662, (f32[768,17,64]{0,2,1:T(8,128)}, f32[3072,2,1088]{0,2,1:T(8,128)}) %tuple.346, (pred[768,768]{0,1:T(8,128)(4,1)}, s32[]{:T(128)}, bf16[3072,1088]{0,1:T(8,128)(2,1)}, bf16[768,17,64]{0,2,1:T(8,128)(2,1)S(1)}, ...), branch_computations={%region_54.54_spmd, %region_55.55_spmd} | conditional | flops 6523404288 | bytes 269411520 | solution.py:306
  1499.5 26.5 %fusion.42 = bf16[768,17,768]{0,2,1:T(8,128)(2,1)} fusion(f32[17,768,768]{2,1,0:T(8,128)} %fusion.225, f32[768,17]{0,1:T(8,128)S(1)} %get-tuple-element.1702, f32[768,17]{0,1:T(8,128)S(1)} %get-tuple-element.1699, pred[768,768]{0,1:T(8,128)(4,1)} %get-tuple-element.1695, bf16[768,17,64]{0,2,1:T(8,128)(2,1)} %bitcast.391, ...), kind=kOutput, calls=%fused_computation.53 | convolution fusion | flops 1343619072 | bytes 64198656 | tf_op jit(solution)/shard_map/while/body/eval_jaxpr/cond/branch_1_fun/qhd,khd->qhk/dot_general | solution.py:271
  1576.9 93.5 %conditional.15 = ((f32[768,17,64]{0,2,1:T(8,128)}, f32[3072,2,1088]{0,2,1:T(8,128)})) conditional(s32[]{:T(128)} %convert_element_type.662, (f32[768,17,64]{0,2,1:T(8,128)}, f32[3072,2,1088]{0,2,1:T(8,128)}) %tuple.346, (pred[768,768]{0,1:T(8,128)(4,1)}, s32[]{:T(128)}, bf16[3072,1088]{0,1:T(8,128)(2,1)}, bf16[768,17,64]{0,2,1:T(8,128)(2,1)S(1)}, ...), branch_computations={%region_54.54_spmd, %region_55.55_spmd} | conditional | flops 6523404288 | bytes 269411520 | solution.py:306
  1596.0 26.5 %fusion.42 = bf16[768,17,768]{0,2,1:T(8,128)(2,1)} fusion(f32[17,768,768]{2,1,0:T(8,128)} %fusion.225, f32[768,17]{0,1:T(8,128)S(1)} %get-tuple-element.1702, f32[768,17]{0,1:T(8,128)S(1)} %get-tuple-element.1699, pred[768,768]{0,1:T(8,128)(4,1)} %get-tuple-element.1695, bf16[768,17,64]{0,2,1:T(8,128)(2,1)} %bitcast.391, ...), kind=kOutput, calls=%fused_computation.53 | convolution fusion | flops 1343619072 | bytes 64198656 | tf_op jit(solution)/shard_map/while/body/eval_jaxpr/cond/branch_1_fun/qhd,khd->qhk/dot_general | solution.py:271
  1707.1 203.7 %while.82 = (s32[]{:T(128)}, f32[768,17,64]{0,2,1:T(8,128)}, f32[3072,2,1088]{0,2,1:T(8,128)}, s32[768]{0:T(1024)S(1)}, s32[1,1,4]{2,1,0:T(1,128)S(1)}, /*index=...) while((s32[]{:T(128)}, f32[768,17,64]{0,2,1:T(8,128)}, ...), condition=%wide.region_43.44_spmd.clone, body=%wide.region_37.43_spmd.clone.sunk | while | flops 6525792768 | bytes 270038496 | solution.py:308
  1710.2 97.7 %conditional.14 = ((f32[768,17,64]{0,2,1:T(8,128)}, f32[3072,2,1088]{0,2,1:T(8,128)})) conditional(s32[]{:T(128)} %convert_element_type.660, (f32[768,17,64]{0,2,1:T(8,128)}, f32[3072,2,1088]{0,2,1:T(8,128)}) %tuple.341, (pred[768,768]{0,1:T(8,128)(4,1)}, s32[]{:T(128)}, bf16[3072,1088]{0,1:T(8,128)(2,1)}, bf16[768,17,64]{0,2,1:T(8,128)(2,1)S(1)}, ...), branch_computations={%region_41.41_spmd, %region_42.42_spmd} | conditional | flops 6523404288 | bytes 269411520 | solution.py:306
  1730.5 27.2 %fusion.31 = bf16[768,17,768]{0,2,1:T(8,128)(2,1)} fusion(f32[17,768,768]{2,1,0:T(8,128)} %fusion.224, f32[768,17]{0,1:T(8,128)S(1)} %get-tuple-element.1676, f32[768,17]{0,1:T(8,128)S(1)} %get-tuple-element.1673, pred[768,768]{0,1:T(8,128)(4,1)} %get-tuple-element.1669, bf16[768,17,64]{0,2,1:T(8,128)(2,1)} %bitcast.392, ...), kind=kOutput, calls=%fused_computation.36 | convolution fusion | flops 1343619072 | bytes 64198656 | tf_op jit(solution)/shard_map/while/body/eval_jaxpr/cond/branch_1_fun/qhd,khd->qhk/dot_general | solution.py:271
  1768.6 18.8 fusion.35
  1813.8 93.7 %conditional.14 = ((f32[768,17,64]{0,2,1:T(8,128)}, f32[3072,2,1088]{0,2,1:T(8,128)})) conditional(s32[]{:T(128)} %convert_element_type.660, (f32[768,17,64]{0,2,1:T(8,128)}, f32[3072,2,1088]{0,2,1:T(8,128)}) %tuple.341, (pred[768,768]{0,1:T(8,128)(4,1)}, s32[]{:T(128)}, bf16[3072,1088]{0,1:T(8,128)(2,1)}, bf16[768,17,64]{0,2,1:T(8,128)(2,1)S(1)}, ...), branch_computations={%region_41.41_spmd, %region_42.42_spmd} | conditional | flops 6523404288 | bytes 269411520 | solution.py:306
  1832.9 26.5 %fusion.31 = bf16[768,17,768]{0,2,1:T(8,128)(2,1)} fusion(f32[17,768,768]{2,1,0:T(8,128)} %fusion.224, f32[768,17]{0,1:T(8,128)S(1)} %get-tuple-element.1676, f32[768,17]{0,1:T(8,128)S(1)} %get-tuple-element.1673, pred[768,768]{0,1:T(8,128)(4,1)} %get-tuple-element.1669, bf16[768,17,64]{0,2,1:T(8,128)(2,1)} %bitcast.392, ...), kind=kOutput, calls=%fused_computation.36 | convolution fusion | flops 1343619072 | bytes 64198656 | tf_op jit(solution)/shard_map/while/body/eval_jaxpr/cond/branch_1_fun/qhd,khd->qhk/dot_general | solution.py:271
  1988.6 249.4 %reduce-scatter.22.cloned.1.call-done = bf16[768,2,1088]{0,2,1:T(8,128)(2,1)} async-done(((bf16[3072,2,1088]{0,2,1:T(8,128)(2,1)}), bf16[768,2,1088]{0,2,1:T(8,128)(2,1)}) %reduce-scatter.22.cloned.1.call-update) | async-done | bytes 3342352 | tf_op jit(solution)/shard_map/reduce_scatter | solution.py:310
  2277.7 18.9 copy.136
  2319.5 30.6 %all-reduce.10 = (bf16[2,1088]{1,0:T(2,128)(2,1)S(1)}, bf16[2,1088]{1,0:T(2,128)(2,1)S(1)}, bf16[2,1088]{1,0:T(2,128)(2,1)S(1)}, bf16[4352]{0:T(1024)(128)(2,1)S(1)}, bf16[2,1088]{1,0:T(2,128)(2,1)S(1)}) all-reduce(bf16[2,1088]{1,0:T(2,128)(2,1)S(1)} %fusion.190, ...), channel_id=4, replica_groups=mesh['dp'=8,'cp'=4] {'dp'}, use_global_device_ids=true, to_apply=%region_64.65.clone | all-reduce | flops 13056 | bytes 52224
  2366.4 137.4 %all-reduce.14.cloned.1.call-done = bf16[1088,3,1088]{2,1,0:T(4,128)(2,1)} async-done(((bf16[1088,3,1088]{2,1,0:T(4,128)(2,1)}), bf16[1088,3,1088]{2,1,0:T(4,128)(2,1)}) %all-reduce.14.cloned.1.call-update) | async-done | bytes 7102480
  2506.6 34.4 %copy.151 = bf16[136,3,1088]{1,0,2:T(8,128)(2,1)} copy(bf16[136,3,1088]{2,1,0:T(4,128)(2,1)} %constant_dynamic-slice_fusion.10) | data formatting | bytes 1775616
  2541.0 35.9 %reshape.823 = bf16[1088,408]{1,0:T(8,128)(2,1)} reshape(bf16[1088,136,3]{2,1,0:T(8,128)(2,1)} %bitcast.386) | data formatting | bytes 1775616
  2586.4 19.0 reduce-scatter.30.cloned.1.call-done
  (664 shorter events, 1158.7 us)
Async XLA Ops:
  7.2 112.6 %all-gather.17.cloned.1.call-start = ((), (), s32[]{:S(2)}) async-start(), calls=%async_computation.8 | async-start | bytes 8460288 | tf_op jit(solution)/shard_map/all_gather | solution.py:59
  9.3 36.7 %copy-start.10 = (bf16[1,2,768,1088]{2,3,1,0:T(8,128)(2,1)S(1)}, bf16[1,2,768,1088]{2,3,1,0:T(8,128)(2,1)}, u32[]{:S(2)}) copy-start(bf16[1,2,768,1088]{2,3,1,0:T(8,128)(2,1)} %param.37) | copy-start | bytes 10027012
  44.5 131.1 %all-gather.35.cloned.1.call-start = ((), (), s32[]{:S(2)}) async-start(), calls=%async_computation.21 | async-start | bytes 1566720 | tf_op jit(solution)/shard_map/all_gather | solution.py:55
  45.2 177.7 %all-gather.27.cloned.1.call-start = ((), (), s32[]{:S(2)}) async-start(), calls=%async_computation.13 | async-start | bytes 1740800 | tf_op jit(solution)/shard_map/all_gather | solution.py:56
  46.0 22.7 copy-start.129
  46.0 211.5 %all-gather.21.cloned.1.call-start = ((), (), s32[]{:S(2)}) async-start(), calls=%async_computation.10 | async-start | bytes 8355840 | tf_op jit(solution)/shard_map/all_gather | solution.py:152
  46.6 86.0 %copy-start.73 = (f32[768]{0:T(1024)}, f32[768]{0:T(1024)S(1)}, u32[]{:S(2)}) copy-start(f32[768]{0:T(1024)S(1)} %get-tuple-element.2163) | copy-start | bytes 9220
  46.6 96.2 %copy-start.75 = (f32[768]{0:T(1024)}, f32[768]{0:T(1024)S(1)}, u32[]{:S(2)}) copy-start(f32[768]{0:T(1024)S(1)} %get-tuple-element.2164) | copy-start | bytes 9220
  47.5 31.6 %copy-start.97 = (f32[768]{0:T(1024)}, f32[768]{0:T(1024)S(1)}, u32[]{:S(2)}) copy-start(f32[768]{0:T(1024)S(1)} %get-tuple-element.1953) | copy-start | bytes 9220
  47.5 31.6 %copy-start.99 = (f32[768]{0:T(1024)}, f32[768]{0:T(1024)S(1)}, u32[]{:S(2)}) copy-start(f32[768]{0:T(1024)S(1)} %get-tuple-element.1954) | copy-start | bytes 9220
  47.5 85.0 %copy-start.85 = (f32[768]{0:T(1024)}, f32[768]{0:T(1024)S(1)}, u32[]{:S(2)}) copy-start(f32[768]{0:T(1024)S(1)} %fusion.195) | copy-start | bytes 9220
  68.7 74.1 %copy-start.87 = (f32[768]{0:T(1024)}, f32[768]{0:T(1024)S(1)}, u32[]{:S(2)}) copy-start(f32[768]{0:T(1024)S(1)} %fusion.193) | copy-start | bytes 9220
  79.7 63.1 %copy-start.65 = (f32[1088]{0:T(1024)}, f32[1088]{0:T(1024)S(1)}, u32[]{:S(2)}) copy-start(f32[1088]{0:T(1024)S(1)} %get-tuple-element.2165) | copy-start | bytes 13060
  79.7 63.1 %copy-start.115 = (f32[1088]{0:T(1024)}, f32[1088]{0:T(1024)S(1)}, u32[]{:S(2)}) copy-start(f32[1088]{0:T(1024)S(1)} %get-tuple-element.1962) | copy-start | bytes 13060
  155.1 177.5 %all-gather.19.cloned.1.call-start = ((), (), s32[]{:S(2)}) async-start(), calls=%async_computation.9 | async-start | bytes 8355840 | tf_op jit(solution)/shard_map/all_gather | solution.py:151
  158.6 306.8 %all-gather.23.cloned.1.call-start = ((), (), s32[]{:S(2)}) async-start(), calls=%async_computation.11 | async-start | bytes 2820096 | tf_op jit(solution)/shard_map/all_gather | solution.py:60
  170.8 302.7 %all-gather.33.cloned.1.call-start = ((), (), s32[]{:S(2)}) async-start(), calls=%async_computation.16 | async-start | bytes 8355840 | tf_op jit(solution)/shard_map/all_gather | solution.py:152
  171.6 346.9 %all-gather.31.cloned.1.call-start = ((), (), s32[]{:S(2)}) async-start(), calls=%async_computation.15 | async-start | bytes 8355840 | tf_op jit(solution)/shard_map/all_gather | solution.py:151
  175.5 595.5 %all-gather.25.cloned.1.call-start = ((), (), s32[]{:S(2)}) async-start(), calls=%async_computation.12 | async-start | bytes 10653696 | tf_op jit(solution)/shard_map/all_gather | solution.py:61
  179.3 683.4 %all-gather.29.cloned.1.call-start = ((), (), s32[]{:S(2)}) async-start(), calls=%async_computation.14 | async-start | bytes 11280384 | tf_op jit(solution)/shard_map/all_gather | solution.py:62
  225.4 832.5 %reduce-scatter.36.cloned.1.call-start = ((), (), s32[]{:S(2)}) async-start(), calls=%async_computation.27 | async-start | bytes 2820096
  470.9 49.7 %copy-start.70 = (f32[768]{0:T(1024)}, f32[768]{0:T(1024)S(1)}, u32[]{:S(2)}) copy-start(f32[768]{0:T(1024)S(1)} %broadcast_multiply_fusion.2) | copy-start | bytes 9220
  472.6 48.0 %copy-start.2 = (bf16[768,1088]{0,1:T(8,128)(2,1)S(1)}, bf16[768,1088]{0,1:T(8,128)(2,1)}, u32[]{:S(2)}) copy-start(bf16[768,1088]{0,1:T(8,128)(2,1)} %get-tuple-element.2120) | copy-start | bytes 5013508
  472.6 48.0 %copy-start.62 = (s32[768]{0:T(1024)S(1)}, s32[768]{0:T(1024)}, u32[]{:S(2)}) copy-start(s32[768]{0:T(1024)} %convert_reduce_fusion.14) | copy-start | bytes 9220
  472.6 48.0 %copy-start.79 = (s32[1,1,4]{2,1,0:T(1,128)S(1)}, s32[1,1,4]{2,1,0:T(1,128)}, u32[]{:S(2)}) copy-start(s32[1,1,4]{2,1,0:T(1,128)} %get-tuple-element.2613) | copy-start | bytes 52
  472.6 48.0 %copy-start.83 = (s32[1,3]{1,0:T(1,128)S(1)}, s32[1,3]{1,0:T(1,128)}, u32[]{:S(2)}) copy-start(s32[1,3]{1,0:T(1,128)} %broadcast_in_dim.386) | copy-start | bytes 40
  473.0 47.6 %copy-start.101 = (f32[768]{0:T(1024)}, f32[768]{0:T(1024)S(1)}, u32[]{:S(2)}) copy-start(f32[768]{0:T(1024)S(1)} %multiply_reduce_fusion.7) | copy-start | bytes 9220
  787.6 75.1 %copy-start.23 = (bf16[1,2,768,1088]{2,3,1,0:T(8,128)(2,1)S(1)}, bf16[1,2,768,1088]{2,3,1,0:T(8,128)(2,1)}, u32[]{:S(2)}) copy-start(bf16[1,2,768,1088]{2,3,1,0:T(8,128)(2,1)} %param.38) | copy-start | bytes 10027012
  896.7 21.8 copy-start.72
  947.3 216.8 %reduce-scatter.28.cloned.1.call-start = ((), (), s32[]{:S(2)}) async-start(), calls=%async_computation.20 | async-start | bytes 11280384 | tf_op jit(solution)/shard_map/reduce_scatter | solution.py:341
  979.5 285.5 %reduce-scatter.26.cloned.1.call-start = ((), (), s32[]{:S(2)}) async-start(), calls=%async_computation.19 | async-start | bytes 10653696 | tf_op jit(solution)/shard_map/reduce_scatter | solution.py:338
  1010.5 153.6 %copy-start.31 = (f32[768,17]{0,1:T(8,128)S(1)}, f32[768,17]{0,1:T(8,128)}, u32[]{:S(2)}) copy-start(f32[768,17]{0,1:T(8,128)} %copy-done.30) | copy-start | bytes 156676
  1010.5 153.6 %copy-start.47 = (f32[768,17]{0,1:T(8,128)S(1)}, f32[768,17]{0,1:T(8,128)}, u32[]{:S(2)}) copy-start(f32[768,17]{0,1:T(8,128)} %copy-done.46) | copy-start | bytes 156676
  1010.5 153.7 %copy-start.59 = (bf16[768,1088]{0,1:T(8,128)(2,1)S(1)}, bf16[768,1088]{0,1:T(8,128)(2,1)}, u32[]{:S(2)}) copy-start(bf16[768,1088]{0,1:T(8,128)(2,1)} %copy-done.58) | copy-start | bytes 5013508
  1010.6 956.7 %reduce-scatter.32.cloned.1.call-start = ((), (), s32[]{:S(2)}) async-start(), calls=%async_computation.23 | async-start | bytes 696320
  1060.0 909.0 %all-reduce.16.cloned.1.call-start = ((), (), s32[]{:S(2)}) async-start(), calls=%async_computation.26 | async-start | bytes 2506752
  1164.1 807.4 %reduce-scatter.34.cloned.1.call-start = ((), (), s32[]{:S(2)}) async-start(), calls=%async_computation.24 | async-start | bytes 2785280
  1268.6 705.0 %reduce-scatter.24.cloned.1.call-start = ((), (), s32[]{:S(2)}) async-start(), calls=%async_computation.18 | async-start | bytes 16711680 | tf_op jit(solution)/shard_map/reduce_scatter | solution.py:310
  1684.4 553.6 %reduce-scatter.22.cloned.1.call-start = ((), (), s32[]{:S(2)}) async-start(), calls=%async_computation.17 | async-start | bytes 16711680 | tf_op jit(solution)/shard_map/reduce_scatter | solution.py:310
  1925.0 578.8 %all-reduce.14.cloned.1.call-start = ((), (), s32[]{:S(2)}) async-start(), calls=%async_computation.25 | async-start | bytes 20054016
  1988.6 253.5 %copy-start.12 = (bf16[1,2,768,1088]{2,3,1,0:T(8,128)(2,1)S(1)}, bf16[1,2,768,1088]{2,3,1,0:T(8,128)(2,1)}, u32[]{:S(2)}) copy-start(bf16[1,2,768,1088]{2,3,1,0:T(8,128)(2,1)} %param.37) | copy-start | bytes 10027012
  1988.6 253.5 %copy-start.66 = (f32[1088]{0:T(1024)S(1)}, f32[1088]{0:T(1024)}, u32[]{:S(2)}) copy-start(f32[1088]{0:T(1024)} %copy-done.65) | copy-start | bytes 13060
  1988.6 253.5 %copy-start.76 = (f32[768]{0:T(1024)S(1)}, f32[768]{0:T(1024)}, u32[]{:S(2)}) copy-start(f32[768]{0:T(1024)} %copy-done.75) | copy-start | bytes 9220
  1988.6 253.5 %copy-start.88 = (f32[768]{0:T(1024)S(1)}, f32[768]{0:T(1024)}, u32[]{:S(2)}) copy-start(f32[768]{0:T(1024)} %copy-done.87) | copy-start | bytes 9220
  1988.6 253.5 %copy-start.116 = (f32[1088]{0:T(1024)S(1)}, f32[1088]{0:T(1024)}, u32[]{:S(2)}) copy-start(f32[1088]{0:T(1024)} %copy-done.115) | copy-start | bytes 13060
  2296.6 308.8 %reduce-scatter.30.cloned.1.call-start = ((), (), s32[]{:S(2)}) async-start(), calls=%async_computation.22 | async-start | bytes 1392640
  2541.0 35.9 %copy-start.90 = (f32[768]{0:T(1024)S(1)}, f32[768]{0:T(1024)}, u32[]{:S(2)}) copy-start(f32[768]{0:T(1024)} %copy-done.89) | copy-start | bytes 9220
  2541.0 35.9 %copy-start.92 = (f32[768]{0:T(1024)S(1)}, f32[768]{0:T(1024)}, u32[]{:S(2)}) copy-start(f32[768]{0:T(1024)} %copy-done.91) | copy-start | bytes 9220
  (122 other events, 831.8 us)
Sparse Core Ops, SparseCore 0:
  44.6 75.1 all-gather.16
  121.6 27.0 all-gather.34
  150.5 31.7 all-gather.26
  184.0 73.4 all-gather.20
  259.2 73.4 all-gather.18
  334.7 32.8 all-gather.22
  370.0 72.4 all-gather.32
  445.0 73.4 all-gather.30
  520.1 90.9 all-gather.24
  612.6 94.0 all-gather.28
  947.4 110.5 reduce-scatter.35
  1060.3 103.7 reduce-scatter.27
  1166.5 98.4 reduce-scatter.25
  1268.5 23.3 reduce-scatter.31
  1294.9 55.8 all-reduce.15
  1353.9 36.5 reduce-scatter.33
  1684.5 126.4 reduce-scatter.23
  1925.1 312.9 reduce-scatter.21
  2296.7 207.0 all-reduce.13
  2577.0 28.2 reduce-scatter.29
where the time goes:
time: 2640 us
  matrix products  1060 us (40%)
  waiting for transfers between devices  846 us (32%)
  local copies, waits for them, and re-layouts  276 us (10%)
  other arithmetic  260 us (10%)
  blocking collectives  155 us (6%)
    reduce_scatter x2, waiting for transfers between devices, per_device(): lax.psum_scatter(back_result[1].astype(jnp.bfloat16), 'cp', scatter_dimen...  249 us
    unnamed x26, waiting for transfers between devices  206 us
    dot_general x6, matrix products, backward_update(): jnp.einsum('qhd,khd->qhk', grad_attended, value_block, preferred_element_...  160 us
    dot_general x6, matrix products, forward_update(): jnp.einsum('qhk,khd->qhd', weights.astype(jnp.bfloat16), value_block, pre...  126 us
    unnamed x270, local copies, waits for them, and re-layouts  126 us
    all_gather x2, waiting for transfers between devices, per_device(): key_rows = lax.all_gather(key_low, 'cp', axis=0, tiled=True)  120 us
    reduce_sum x6, other arithmetic, forward_update(): weight_sum = weight_sum * factor + jnp.sum(weights, axis=-1)  106 us
    dot_general x6, matrix products, backward_update(): jnp.einsum('qhk,qhd->khd', probs.astype(jnp.bfloat16), grad_attended, pre...  105 us
  transfers between devices with their start and end apart: 20, of which 10 were waited for; matrix products, arithmetic and copies ran while one was open for 50% of the time, Pallas kernels for 0%

commit v1 on v0

v1 whole, which is shorter than its diff:
```python
import functools

import jax
import jax.numpy as jnp
from jax import lax
from jax.experimental.layout import Layout, with_layout_constraint
from jax.experimental import pallas as pl
from jax.experimental.pallas import tpu as pltpu
from jax.sharding import PartitionSpec as P

HEAD_DIM = 64
PAIR = 2 * HEAD_DIM
EPS = 1e-05
NEG = -1e30
TILE = 256
LOOK = 3
EXTRA = 16
VMEM_LIMIT = 56 * 1024 * 1024
UP_ROWS = 768
UP_COLS = 256
PEAK = 1.1535e15


def cost(micros, *reads):
    size = sum(item.size * item.dtype.itemsize for item in reads)
    return pl.CostEstimate(flops=int(micros * 1e-6 * PEAK), bytes_accessed=size, transcendentals=0)


def nt(a, b):
    return lax.dot_general(a, b, (((1,), (1,)), ((), ())), preferred_element_type=jnp.float32)


def nn(a, b):
    return lax.dot_general(a, b, (((1,), (0,)), ((), ())), preferred_element_type=jnp.float32)


def lanes(slot, kind):
    start = (3 * slot + kind) * PAIR
    return slice(start, start + PAIR)


def forward_kernel(tile, heads, rowat, low, mid, qkv_ref, first_ref, out_ref, lse_ref, vt_scr):
    total = qkv_ref.shape[0]
    tiles = total // tile
    slots = (heads + 1) // 2
    left = lax.broadcasted_iota(jnp.int32, (1, PAIR), 1) < HEAD_DIM

    def prepare(t, _):
        at = pl.multiple_of(rowat[t], tile)
        to = pl.multiple_of(t * tile, tile)
        for s in range(slots):
            value = qkv_ref[pl.ds(at, tile), lanes(s, 2)].astype(jnp.float32).T
            for h in range(2 * s, min(2 * s + 2, heads)):
                half = value[(h % 2) * HEAD_DIM : (h % 2 + 1) * HEAD_DIM]
                vt_scr[h, 0:HEAD_DIM, pl.ds(to, tile)] = half.astype(jnp.bfloat16)
                vt_scr[h, HEAD_DIM:, pl.ds(to, tile)] = jnp.ones((EXTRA, tile), jnp.bfloat16)
        return 0

    lax.fori_loop(0, tiles, prepare, 0)

    def query_step(t, _):
        at = pl.multiple_of(rowat[t], tile)
        to = pl.multiple_of(t * tile, tile)
        queries = []
        for s in range(slots):
            query = qkv_ref[pl.ds(at, tile), lanes(s, 0)] * jnp.asarray(HEAD_DIM**-0.5, jnp.bfloat16)
            zero = jnp.zeros_like(query)
            queries += [jnp.where(left, query, zero), jnp.where(left, zero, query)]

        def visit(masked, j, carry):
            start = pl.multiple_of(rowat[j], tile)
            there = pl.multiple_of(j * tile, tile)
            if masked:
                places = j * tile + lax.broadcasted_iota(jnp.int32, (tile, tile), 0)
                own = t * tile + lax.broadcasted_iota(jnp.int32, (tile, tile), 1)
                allowed = (places >= first_ref[0:1, pl.ds(to, tile)]) & (places <= own)
            def score(h):
                return nt(qkv_ref[pl.ds(start, tile), lanes(h // 2, 1)], queries[h])

            new = []
            ahead = [score(h) for h in range(min(LOOK, heads))]
            for h in range(heads):
                if h + LOOK < heads:
                    ahead.append(score(h + LOOK))
                top, acc = carry[2 * h], carry[2 * h + 1]
                scores = ahead[h]
                if masked:
                    scores = jnp.where(allowed, scores, NEG)
                fresh = jnp.maximum(top, jnp.max(scores, axis=0, keepdims=True))
                weights = jnp.exp(scores - fresh).astype(jnp.bfloat16)
                factor = jnp.exp(top - fresh)
                acc = acc * factor + nn(vt_scr[h, :, pl.ds(there, tile)], weights)
                new += [fresh, acc]
            return tuple(new)

        carry = (
            jnp.full((1, tile), NEG, jnp.float32),
            jnp.zeros((HEAD_DIM + EXTRA, tile), jnp.float32),
        ) * heads
        edges = mid[t] - low[t]
        carry = lax.fori_loop(mid[t], t, functools.partial(visit, False), carry)
        carry = lax.fori_loop(
            0,
            edges + 1,
            lambda i, c: visit(True, jnp.where(i < edges, low[t] + i, t), c),
            carry,
        )
        for s in range(slots):
            outs = []
            for h in (2 * s, 2 * s + 1):
                if h < heads:
                    weight_sum = carry[2 * h + 1][HEAD_DIM : HEAD_DIM + 1]
                    outs.append(carry[2 * h + 1][:HEAD_DIM] / weight_sum)
                    lse_ref[h : h + 1, pl.ds(to, tile)] = carry[2 * h] + jnp.log(weight_sum)
                else:
                    outs.append(jnp.zeros((HEAD_DIM, tile), jnp.float32))
            joined = jnp.concatenate(outs, axis=0).T
            out_ref[pl.ds(at, tile), s * PAIR : (s + 1) * PAIR] = joined.astype(out_ref.dtype)
        return 0

    lax.fori_loop(0, tiles, query_step, 0)


def attention_forward(qkv, rowat, low, mid, first, tile, heads):
    total = qkv.shape[0]
    slots = (heads + 1) // 2
    smem = pl.BlockSpec(memory_space=pltpu.SMEM)
    vmem = pl.BlockSpec(memory_space=pltpu.VMEM)
    return pl.pallas_call(
        functools.partial(forward_kernel, tile, heads),
        in_specs=[smem, smem, smem, vmem, vmem],
        out_specs=[vmem, vmem],
        out_shape=[
            jax.ShapeDtypeStruct((total, slots * PAIR), jnp.bfloat16),
            jax.ShapeDtypeStruct((heads, total), jnp.float32),
        ],
        scratch_shapes=[pltpu.VMEM((heads, HEAD_DIM + EXTRA, total), jnp.bfloat16)],
        compiler_params=pltpu.CompilerParams(vmem_limit_bytes=VMEM_LIMIT),
        cost_estimate=cost(74, qkv),
        name="attention_forward",
    )(rowat, low, mid, qkv, first)


def backward_kernel(
    tile, heads, rowat, full, high, qkv_ref, do_ref, o_ref, first_ref, lse_ref, out_ref, dq_scr, delta_scr
):
    total = qkv_ref.shape[0]
    tiles = total // tile
    slots = (heads + 1) // 2
    left = lax.broadcasted_iota(jnp.int32, (1, PAIR), 1) < HEAD_DIM
    scale = HEAD_DIM**-0.5

    def prepare(t, _):
        at = pl.multiple_of(rowat[t], tile)
        to = pl.multiple_of(t * tile, tile)
        for s in range(slots):
            part = slice(s * PAIR, (s + 1) * PAIR)
            product = do_ref[pl.ds(at, tile), part].astype(jnp.float32) * o_ref[
                pl.ds(at, tile), part
            ].astype(jnp.float32)
            flip = product.T
            for h in range(2 * s, min(2 * s + 2, heads)):
                half = flip[(h % 2) * HEAD_DIM : (h % 2 + 1) * HEAD_DIM]
                delta_scr[h : h + 1, pl.ds(to, tile)] = jnp.sum(half, axis=0, keepdims=True)
        dq_scr[:, pl.ds(to, tile)] = jnp.zeros((slots * PAIR, tile), jnp.float32)
        return 0

    lax.fori_loop(0, tiles, prepare, 0)

    def key_step(j, _):
        at = pl.multiple_of(rowat[j], tile)
        keys_t = []
        for s in range(slots):
            flip = qkv_ref[pl.ds(at, tile), lanes(s, 1)].astype(jnp.float32).T.astype(jnp.bfloat16)
            keys_t += [flip[:HEAD_DIM], flip[HEAD_DIM:]]

        def visit(masked, t, carry):
            start = pl.multiple_of(rowat[t], tile)
            to = pl.multiple_of(t * tile, tile)
            if masked:
                places = j * tile + lax.broadcasted_iota(jnp.int32, (tile, tile), 0)
                own = t * tile + lax.broadcasted_iota(jnp.int32, (tile, tile), 1)
                allowed = (places >= first_ref[0:1, pl.ds(to, tile)]) & (places <= own)
            def products(h):
                s = h // 2
                keep = left if h % 2 == 0 else ~left
                pair_query = qkv_ref[pl.ds(start, tile), lanes(s, 0)] * jnp.asarray(scale, jnp.bfloat16)
                pair_grad = do_ref[pl.ds(start, tile), s * PAIR : (s + 1) * PAIR]
                query = jnp.where(keep, pair_query, jnp.zeros_like(pair_query))
                grad = jnp.where(keep, pair_grad, jnp.zeros_like(pair_grad))
                scores = nt(qkv_ref[pl.ds(at, tile), lanes(s, 1)], query)
                grad_probs = nt(qkv_ref[pl.ds(at, tile), lanes(s, 2)], grad)
                return query, grad, scores, grad_probs

            new = list(carry)
            ahead = [products(h) for h in range(min(LOOK, heads))]
            for h in range(heads):
                if h + LOOK < heads:
                    ahead.append(products(h + LOOK))
                query, grad, scores, grad_probs = ahead[h]
                s = h // 2
                probs = jnp.exp(scores - lse_ref[h : h + 1, pl.ds(to, tile)])
                if masked:
                    probs = jnp.where(allowed, probs, 0.0)
                grad_scores = probs * (grad_probs - delta_scr[h : h + 1, pl.ds(to, tile)])
                grad_scores = grad_scores.astype(jnp.bfloat16)
                new[2 * s + 1] = new[2 * s + 1] + nn(probs.astype(jnp.bfloat16), grad)
                new[2 * s] = new[2 * s] + nn(grad_scores, query)
                here = slice(h * HEAD_DIM, (h + 1) * HEAD_DIM)
                dq_scr[here, pl.ds(to, tile)] += nn(keys_t[h], grad_scores)
            return tuple(new)

        carry = (jnp.zeros((tile, PAIR), jnp.float32),) * (2 * slots)
        carry = lax.fori_loop(j + 1, full[j], functools.partial(visit, False), carry)
        carry = lax.fori_loop(
            0,
            high[j] - full[j] + 1,
            lambda i, c: visit(True, jnp.where(i == 0, j, full[j] + i - 1), c),
            carry,
        )
        for s in range(slots):
            out_ref[pl.ds(at, tile), lanes(s, 1)] = carry[2 * s].astype(out_ref.dtype)
            out_ref[pl.ds(at, tile), lanes(s, 2)] = carry[2 * s + 1].astype(out_ref.dtype)
        return 0

    lax.fori_loop(0, tiles, key_step, 0)

    def finish(t, _):
        at = pl.multiple_of(rowat[t], tile)
        to = pl.multiple_of(t * tile, tile)
        for s in range(slots):
            grad = dq_scr[s * PAIR : (s + 1) * PAIR, pl.ds(to, tile)].T * scale
            out_ref[pl.ds(at, tile), lanes(s, 0)] = grad.astype(out_ref.dtype)
        return 0

    lax.fori_loop(0, tiles, finish, 0)


def attention_backward(qkv, grad, out, rowat, full, high, first, lse, tile, heads):
    total = qkv.shape[0]
    slots = (heads + 1) // 2
    smem = pl.BlockSpec(memory_space=pltpu.SMEM)
    vmem = pl.BlockSpec(memory_space=pltpu.VMEM)
    return pl.pallas_call(
        functools.partial(backward_kernel, tile, heads),
        in_specs=[smem, smem, smem, vmem, vmem, vmem, vmem, vmem],
        out_specs=vmem,
        out_shape=jax.ShapeDtypeStruct(qkv.shape, jnp.bfloat16),
        scratch_shapes=[
            pltpu.VMEM((slots * PAIR, total), jnp.float32),
            pltpu.VMEM((heads, total), jnp.float32),
        ],
        compiler_params=pltpu.CompilerParams(vmem_limit_bytes=VMEM_LIMIT),
        cost_estimate=cost(116, qkv),
        name="attention_backward",
    )(rowat, full, high, qkv, grad, out, first, lse)


def up_kernel(x_ref, w_ref, b_ref, active_ref, slope_ref):
    cols = w_ref.shape[2]
    cuts = [slice(at, min(at + UP_COLS, cols)) for at in range(0, cols, UP_COLS)]
    rows = x_ref[...]
    ahead = [nn(rows, w_ref[0, :, cut]) for cut in cuts[:1]]
    for k, cut in enumerate(cuts):
        if k + 1 < len(cuts):
            ahead.append(nn(rows, w_ref[0, :, cuts[k + 1]]))
        upper = ahead[k] + b_ref[0, :, cut]
        size = jnp.abs(upper)
        below = 1.0 + (0.3275911 * 0.7071067811865476) * size
        t = pl.reciprocal(below, approx=True)
        t = t * (2.0 - below * t)
        poly = 0.5 * 1.061405429
        for term in (-1.453152027, 1.421413741, -0.284496736, 0.254829592):
            poly = poly * t + 0.5 * term
        bell = jnp.exp2((upper * upper) * (-0.5 * 1.4426950408889634))
        tail = (poly * t) * bell
        normal = jnp.where(upper >= 0, 1.0 - tail, tail)
        active_ref[0, :, cut] = (upper * normal).astype(active_ref.dtype)
        slope_ref[0, :, cut] = (normal + upper * bell * 0.3989422804014327).astype(slope_ref.dtype)


def up_forward(rows, weight, bias):
    total, width = rows.shape
    slabs, _, cols = weight.shape
    span = next(size for size in (UP_ROWS, 192, 64, 16) if total % size == 0)
    out = jax.ShapeDtypeStruct((slabs, total, cols), jnp.bfloat16)
    return pl.pallas_call(
        up_kernel,
        grid=(slabs, total // span),
        in_specs=[
            pl.BlockSpec((span, width), lambda c, r: (r, 0)),
            pl.BlockSpec((1, width, cols), lambda c, r: (c, 0, 0)),
            pl.BlockSpec((1, 1, cols), lambda c, r: (c, 0, 0)),
        ],
        out_specs=[pl.BlockSpec((1, span, cols), lambda c, r: (c, r, 0))] * 2,
        out_shape=[out, out],
        compiler_params=pltpu.CompilerParams(vmem_limit_bytes=VMEM_LIMIT),
        cost_estimate=cost(30, rows, weight),
        name="up_forward",
    )(rows, weight, bias)


def norm_kernel(x_ref, gain_ref, shift_ref, out_ref):
    rows = x_ref[...].astype(jnp.float32)
    center = rows - jnp.mean(rows, axis=-1, keepdims=True)
    spread = jnp.mean(center * center, axis=-1, keepdims=True)
    rows = center * lax.rsqrt(spread + EPS) * gain_ref[...] + shift_ref[...]
    out_ref[...] = rows.astype(out_ref.dtype)


def norm_rows(rows, gain, shift):
    total, width = rows.shape
    span = next(size for size in (384, 192, 64, 16) if total % size == 0)
    vector = pl.BlockSpec((1, width), lambda r: (0, 0))
    block = pl.BlockSpec((span, width), lambda r: (r, 0))
    return pl.pallas_call(
        norm_kernel,
        grid=(total // span,),
        in_specs=[block, vector, vector],
        out_specs=block,
        out_shape=jax.ShapeDtypeStruct(rows.shape, jnp.bfloat16),
        compiler_params=pltpu.CompilerParams(vmem_limit_bytes=VMEM_LIMIT),
        cost_estimate=cost(8, rows),
        name="norm_rows",
    )(rows, gain[None], shift[None])


def merge_kernel(x_ref, out_ref):
    pieces = [x_ref[0, k].astype(jnp.float32) for k in range(x_ref.shape[1])]
    out_ref[0] = jnp.concatenate(pieces, axis=1).astype(out_ref.dtype)


def merge_lanes(values):
    slabs, pieces, rows, cols = values.shape
    if pieces == 1:
        return values[:, 0]
    span = next(size for size in (272, 64, 16, rows) if rows % size == 0)
    return pl.pallas_call(
        merge_kernel,
        grid=(slabs, rows // span),
        in_specs=[pl.BlockSpec((1, pieces, span, cols), lambda c, r: (c, 0, r, 0))],
        out_specs=pl.BlockSpec((1, span, pieces * cols), lambda c, r: (c, r, 0)),
        out_shape=jax.ShapeDtypeStruct((slabs, rows, pieces * cols), values.dtype),
        compiler_params=pltpu.CompilerParams(vmem_limit_bytes=VMEM_LIMIT),
        cost_estimate=cost(8, values),
        name="merge_lanes",
    )(values)


def pack_lanes(columns):
    cols = columns[0].shape[1]
    whole = cols // PAIR * PAIR
    pieces = [item[:, at : at + PAIR] for item in columns for at in range(0, whole, PAIR)]
    if cols > whole:
        rest = jnp.concatenate([item[:, whole:] for item in columns], axis=1)
        spare = -rest.shape[1] % PAIR
        rest = jnp.concatenate((rest, jnp.zeros((rest.shape[0], spare), rest.dtype)), axis=1)
        pieces += [rest[:, at : at + PAIR] for at in range(0, rest.shape[1], PAIR)]
    return pieces


def unpack_lanes(pieces, cols):
    count = cols // PAIR
    left = cols - count * PAIR
    rest = jnp.concatenate(pieces[3 * count :], axis=1) if left else None
    return [
        jnp.concatenate(
            list(pieces[k * count : (k + 1) * count]) + ([rest[:, k * left : (k + 1) * left]] if left else []),
            axis=1,
        )
        for k in range(3)
    ]


def mix_take_kernel(main, parts, cols, part_ref, x_ref, out_ref):
    part = part_ref[0]
    slots = main // PAIR
    shards = [
        unpack_lanes([x_ref[c, 0, k].astype(jnp.float32) for k in range(x_ref.shape[2])], cols)
        for c in range(x_ref.shape[0])
    ]
    for kind in range(3):
        full = jnp.concatenate([shard[kind] for shard in shards], axis=1)
        own = full[:, :main]
        for k in range(1, parts):
            own = jnp.where(part == k, full[:, k * main : (k + 1) * main], own)
        last = full[:, parts * main :]
        last = jnp.where(part == 0, last, 0.0)
        last = jnp.concatenate((last, jnp.zeros_like(last)), axis=1)
        for s in range(slots + 1):
            piece = own[:, s * PAIR : (s + 1) * PAIR] if s < slots else last
            out_ref[0, :, lanes(s, kind)] = piece.astype(out_ref.dtype)


def mix_take(shards, part, main, parts, cols):
    ncp, ndp, pieces, rows, _ = shards.shape
    width = 3 * (main + PAIR)
    return pl.pallas_call(
        functools.partial(mix_take_kernel, main, parts, cols),
        grid=(ndp,),
        in_specs=[
            pl.BlockSpec(memory_space=pltpu.SMEM),
            pl.BlockSpec((ncp, 1, pieces, rows, PAIR), lambda d: (0, d, 0, 0, 0)),
        ],
        out_specs=pl.BlockSpec((1, rows, width), lambda d: (d, 0, 0)),
        out_shape=jax.ShapeDtypeStruct((ndp, rows, width), shards.dtype),
        compiler_params=pltpu.CompilerParams(vmem_limit_bytes=VMEM_LIMIT),
        cost_estimate=cost(8, shards),
        name="mix_take",
    )(part.reshape(1), shards)


def mix_spread_kernel(main, parts, cols, at_ref, x_ref, keep_ref, send_ref):
    part, core = at_ref[0], at_ref[1]
    slots = main // PAIR
    for out_ref, row in ((keep_ref, core), (send_ref, 1 - core)):
        kinds = []
        for kind in range(3):
            pieces = [x_ref[row, :, lanes(s, kind)].astype(jnp.float32) for s in range(slots + 1)]
            own = jnp.concatenate(pieces[:slots], axis=1)
            last = pieces[slots][:, :HEAD_DIM]
            full = [jnp.where(part == k, own, 0.0) for k in range(parts)]
            full.append(jnp.where(part == 0, last, 0.0))
            kinds.append(jnp.concatenate(full, axis=1))
        for c in range(out_ref.shape[1]):
            packed = pack_lanes([full[:, c * cols : (c + 1) * cols] for full in kinds])
            for k, piece in enumerate(packed):
                out_ref[0, c, k] = piece.astype(out_ref.dtype)


def mix_spread(grad, part, core, main, parts, ncp):
    ndp, rows, width = grad.shape
    cols = (parts * main + HEAD_DIM) // ncp
    pieces = 3 * (cols // PAIR) + -(-3 * (cols % PAIR) // PAIR)
    out = jax.ShapeDtypeStruct((ndp // 2, ncp, pieces, rows, PAIR), grad.dtype)
    return pl.pallas_call(
        functools.partial(mix_spread_kernel, main, parts, cols),
        grid=(ndp // 2,),
        in_specs=[
            pl.BlockSpec(memory_space=pltpu.SMEM),
            pl.BlockSpec((2, rows, width), lambda d: (d, 0, 0)),
        ],
        out_specs=[pl.BlockSpec((1, ncp, pieces, rows, PAIR), lambda d: (d, 0, 0, 0, 0))] * 2,
        out_shape=[out, out],
        compiler_params=pltpu.CompilerParams(vmem_limit_bytes=VMEM_LIMIT),
        cost_estimate=cost(8, grad),
        name="mix_spread",
    )(jnp.stack((part, core)), grad)


def pack_tables(order_row, lengths, rows, tile):
    blocks = order_row.shape[0]
    total = blocks * rows
    tiles = total // tile
    places = jnp.arange(total, dtype=jnp.int32)
    ends = jnp.cumsum(lengths, dtype=jnp.int32)
    begins = ends - lengths
    seq = jnp.sum((places[:, None] >= ends[None, :]).astype(jnp.int32), axis=1)
    pick = seq[:, None] == jnp.arange(lengths.shape[0], dtype=jnp.int32)[None, :]
    first = jnp.sum(jnp.where(pick, begins[None, :], 0), axis=1)
    last = jnp.sum(jnp.where(pick, ends[None, :], 0), axis=1) - 1
    index = jnp.arange(tiles, dtype=jnp.int32)
    per = rows // tile
    holder = holders(order_row)
    slots = jnp.arange(blocks, dtype=jnp.int32)
    held = (index // per)[:, None] == slots[None, :]
    rowat = jnp.sum(jnp.where(held, holder[None, :], 0), axis=1) * rows + (index % per) * tile
    firsts = first.reshape(tiles, tile)
    lasts = last.reshape(tiles, tile)
    low = firsts[:, 0] // tile
    mid = jnp.minimum((firsts[:, -1] + tile - 1) // tile, index)
    high = lasts[:, -1] // tile + 1
    full = jnp.clip((lasts[:, 0] + 1) // tile, index + 1, high)
    return rowat, low, mid, full, high, first[None]


def holders(order_row):
    slots = jnp.arange(order_row.shape[0], dtype=jnp.int32)
    return jnp.sum(
        jnp.where(order_row[None, :] == slots[:, None], slots[None, :], 0), axis=1, dtype=jnp.int32
    )


def low(values):
    return values.astype(jnp.bfloat16)


def wide(values):
    return values.astype(jnp.float32)


def row_major(values):
    return with_layout_constraint(values, Layout(tuple(range(values.ndim))))


def normalize(rows):
    center = rows - jnp.mean(rows, axis=-1, keepdims=True)
    rstd = lax.rsqrt(jnp.mean(center * center, axis=-1, keepdims=True) + EPS)
    return center * rstd, rstd


def normalize_back(grad, gain, xhat, rstd):
    scaled = grad * gain
    mean = jnp.mean(scaled, axis=-1, keepdims=True)
    slope = jnp.mean(scaled * xhat, axis=-1, keepdims=True)
    return rstd * (scaled - mean - xhat * slope)


def flip_bit(values, axis, place):
    return lax.ppermute(values, axis, [(i, i ^ (1 << place)) for i in range(lax.axis_size(axis))])


def halve(values, bits, bit):
    at = bits.index(bit)
    axis, place = bit
    own = (lax.axis_index(axis) >> place) & 1
    send = lax.dynamic_index_in_dim(values, 1 - own, at, keepdims=False)
    keep = lax.dynamic_index_in_dim(values, own, at, keepdims=False)
    got = flip_bit(send, axis, place)
    return (wide(keep) + wide(got)).astype(values.dtype), bits[:at] + bits[at + 1 :]


def bits_of(axis):
    return tuple((axis, place) for place in reversed(range(lax.axis_size(axis).bit_length() - 1)))


def split_bits(values, lead, bits):
    return values.reshape((2,) * len(bits) + values.shape[lead:])


def tie(*values):
    return lax.optimization_barrier(values)


def begin(values, bits):
    cut = min((values.shape[-2] // 2 + 7) // 8 * 8, values.shape[-2])
    near = sorted(bit for bit in bits if bit[0] == "cp")
    far = sorted(bit for bit in bits if bit[0] == "dp")
    halves = (values[..., :cut, :], near + far), (values[..., cut:, :], near[::-1] + far)
    return [(piece, bits, order) for piece, order in halves if piece.shape[-2]]


def step(state):
    done = []
    for piece, left, order in state:
        if order:
            piece, left = halve(piece, left, order[0])
        done.append((piece, left, order[1:]))
    return done


def held(state):
    return [piece for piece, _, _ in state]


def placed(state, pieces):
    return [(piece,) + item[1:] for piece, item in zip(pieces, state)]


def finish(state):
    while any(order for _, _, order in state):
        state = step(state)
    return wide(jnp.concatenate(held(state), axis=-2))


def flip_role(values, place):
    ndp, ncp = lax.axis_size("dp"), lax.axis_size("cp")
    pairs = []
    for d in range(ndp):
        bit = 1 << (place if d % 2 == 0 else 1 - place)
        pairs += [(d * ncp + c, d * ncp + (c ^ bit)) for c in range(ncp)]
    return lax.ppermute(values, ("dp", "cp"), pairs)


def role_of(index):
    swapped = (index >> 1) | ((index & 1) << 1)
    return jnp.where(lax.axis_index("dp") % 2 == 0, index, swapped)


def gather_pack(values, mine, crossed):
    own = lax.dynamic_index_in_dim(values, mine, 0, keepdims=False)
    if crossed:
        other = lax.dynamic_index_in_dim(values, 1 - mine, 0, keepdims=False)
        beside = flip_role(own, 0)
        below = flip_role(other, 1)
        return jnp.stack((own, beside, below, flip_role(below, 0)))
    whole = lax.all_gather(values, "cp", axis=0)
    return lax.dynamic_index_in_dim(whole, mine, 1, keepdims=False)


def scatter_pack(values, mine, micro, crossed):
    if crossed:
        own = low(wide(values[0]) + wide(flip_role(values[1], 0)))
        below = low(wide(values[2]) + wide(flip_role(values[3], 0)))
        other = flip_role(below, 1)
        first = mine == 0
        return jnp.stack((jnp.where(first, own, other), jnp.where(first, other, own)))
    slots = jnp.arange(micro, dtype=jnp.int32)
    spread = jnp.where((slots == mine)[None, :, None, None], values[:, None], jnp.zeros((), values.dtype))
    return lax.psum_scatter(spread, "cp", scatter_dimension=0, tiled=False)


def heads_to_rows(values, mine, part, micro, parts, crossed):
    _, rows, width = values.shape
    if crossed:
        got = (
            values[0],
            flip_role(values[1], 0),
            flip_role(values[2], 1),
            lax.ppermute(values[3], "cp", [(i, i ^ 3) for i in range(4)]),
        )
        first = part == 0
        pair = [
            jnp.concatenate((jnp.where(first, a, b), jnp.where(first, b, a)), axis=1)
            for a, b in ((got[0], got[1]), (got[2], got[3]))
        ]
        first = mine == 0
        return jnp.stack((jnp.where(first, pair[0], pair[1]), jnp.where(first, pair[1], pair[0])))
    got = lax.all_to_all(values, "cp", 0, 0, tiled=True).reshape(micro, parts, rows, width)
    return got.transpose(0, 2, 1, 3).reshape(micro, rows, parts * width)


def rows_to_heads(values, mine, part, micro, parts, crossed):
    _, rows, width = values.shape
    width = width // parts
    if crossed:
        first = mine == 0
        own = jnp.where(first, values[0], values[1])
        other = jnp.where(first, values[1], values[0])
        first = part == 0
        pieces = []
        for item in (own, other):
            a, b = item[:, :width], item[:, width:]
            pieces += [jnp.where(first, a, b), jnp.where(first, b, a)]
        return jnp.stack((
            pieces[0],
            flip_role(pieces[1], 0),
            flip_role(pieces[2], 1),
            lax.ppermute(pieces[3], "cp", [(i, i ^ 3) for i in range(4)]),
        ))
    cut = values.reshape(micro, rows, parts, width).transpose(0, 2, 1, 3)
    return lax.all_to_all(cut.reshape(micro * parts, rows, width), "cp", 0, 0, tiled=True)


def per_device(
    tokens,
    cotangent,
    seq_lengths,
    block_order,
    norm_gain,
    norm_shift,
    mix_weight,
    mix_bias,
    out_weight,
    up_weight,
    up_bias,
    down_weight,
    out_bias,
):
    micro, rows, width = tokens.shape[1:]
    ndp, ncp = lax.axis_size("dp"), lax.axis_size("cp")
    device = lax.axis_index("cp")
    parts = ncp // micro
    crossed = ncp == 4 and micro == 2 and rows % TILE == 0
    role = role_of(device) if crossed else device
    mine, part = role // parts, role % parts
    core_index = lax.axis_index("dp") % 2
    heads = width // HEAD_DIM
    per = heads // 2 // parts
    slots = per + 1
    own_heads = 2 * per + 1
    main = per * PAIR
    odd = width - HEAD_DIM
    ff = down_weight.shape[0] * ndp
    cells = width // ndp
    count = micro * rows
    total = ncp * rows

    def gather(shard, axes):
        return lax.all_gather(shard, axes, axis=0, tiled=False)

    tokens = row_major(tokens)
    cotangent = row_major(cotangent)
    small = jnp.concatenate(
        [item.reshape(1, -1) for item in (norm_gain, norm_shift, mix_bias, out_bias, up_bias)],
        axis=1,
    )
    small = wide(lax.all_gather(small, "dp", axis=0, tiled=True))
    gains, shifts, mix_biases, out_biases = (
        small[:, k * 2 * cells : (k + 1) * 2 * cells]
        .reshape(ndp, 2, cells)
        .transpose(1, 0, 2)
        .reshape(2, width)
        for k in range(4)
    )
    up_biases = small[:, 8 * cells :].reshape(-1)

    pack = gather_pack(tokens[0], mine, crossed)
    mix_all = gather(
        jnp.stack(pack_lanes([mix_weight[:, k] for k in range(3)])), ("cp", "dp")
    )
    out_all = gather(out_weight, ("cp", "dp"))
    up_all = gather(up_weight, ("cp", "dp"))
    down_all = gather(down_weight.T, ("dp", "cp"))
    mix_own = mix_take(
        mix_all.reshape((ncp, ndp) + mix_all.shape[1:]), part, main, parts, width // ncp
    )
    mix_own = mix_own.reshape(width, -1)
    out_full = merge_lanes(out_all.reshape(1, ncp, width, -1))[0]
    up_slabs = up_all.reshape(ncp, width, ff // ncp)
    down_slabs = merge_lanes(down_all.reshape(ncp, ndp // ncp, width, -1))

    def own_columns(values):
        head = lax.dynamic_slice_in_dim(values, part * main, main, values.ndim - 1)
        last = jnp.where(part == 0, values[..., odd:], jnp.zeros((), values.dtype))
        return jnp.concatenate((head, last, jnp.zeros_like(last)), axis=-1)

    def from_own_columns(values):
        blank = jnp.zeros(values.shape[:-1] + (odd,), values.dtype)
        last = jnp.where(part == 0, values[..., main : main + HEAD_DIM], jnp.zeros((), values.dtype))
        spread = lax.dynamic_update_slice_in_dim(blank, values[..., :main], part * main, values.ndim - 1)
        return jnp.concatenate((spread, last), axis=-1)

    def slot_major(values):
        lead = values.shape[:-2]
        cut = values.reshape(lead + (3, slots, PAIR))
        return jnp.swapaxes(cut, -3, -2).reshape(lead + (slots * 3 * PAIR,))

    def kind_major(values):
        lead = values.shape[:-1]
        cut = values.reshape(lead + (slots, 3, PAIR))
        return jnp.swapaxes(cut, -3, -2).reshape(lead + (3, slots * PAIR))

    order_row = lax.dynamic_index_in_dim(block_order[0], mine, 0, keepdims=False)
    lengths = lax.dynamic_index_in_dim(seq_lengths[0], mine, 0, keepdims=False)
    places = jnp.arange(ncp, dtype=jnp.int32)
    if crossed:
        relative = places[:, None] == role_of(places ^ role)[None, :]
        kept_order = jnp.sum(jnp.where(relative, order_row[:, None], 0), axis=0, dtype=jnp.int32)
        tables = pack_tables(kept_order, lengths, rows, TILE)
    else:
        pack = jnp.take(pack, holders(order_row), axis=0)
        tables = pack_tables(jnp.zeros((1,), jnp.int32), lengths, total, TILE)
    rowat, tile_low, tile_mid, tile_full, tile_high, first = tables

    def to_devices(values):
        values = values.reshape(ncp, rows, -1)
        return values if crossed else jnp.take(values, order_row, axis=0)

    def to_places(values):
        values = values if crossed else jnp.take(values, holders(order_row), axis=0)
        return values.reshape(total, -1)

    pack, mix_own = tie(pack, mix_own)
    pack_low = norm_rows(pack.reshape(total, width), gains[0], shifts[0])
    bias_own = slot_major(
        own_columns(jnp.stack((mix_biases[0], jnp.zeros((width,), jnp.float32), mix_biases[1])))
    )
    mixed = low(jnp.dot(pack_low, mix_own, preferred_element_type=jnp.float32) + bias_own)
    attended_own, log_sums = attention_forward(
        mixed, rowat, tile_low, tile_mid, first, TILE, own_heads
    )
    attended = heads_to_rows(to_devices(attended_own), mine, part, micro, parts, crossed)
    attended = attended.reshape(count, parts * slots * PAIR)

    pieces = []
    for k in range(parts):
        pieces.append(out_full[k * main : (k + 1) * main])
        last = out_full[odd:] if k == 0 else jnp.zeros((HEAD_DIM, width), jnp.bfloat16)
        pieces += [last, jnp.zeros((HEAD_DIM, width), jnp.bfloat16)]
    out_own = jnp.concatenate(pieces, axis=0)

    source = wide(tokens[0].reshape(count, width))
    residual = (
        source + jnp.dot(attended, out_own, preferred_element_type=jnp.float32) + out_biases[0]
    )
    hat2, rstd2 = normalize(residual)
    normed2 = low(hat2 * gains[1] + shifts[1])
    active, slope = up_forward(normed2, up_slabs, up_biases.reshape(ncp, 1, ff // ncp))
    result = (
        residual
        + jnp.einsum("ctf,cdf->td", active, down_slabs, preferred_element_type=jnp.float32)
        + out_biases[1]
    )
    layer_out = low(result).reshape(1, micro, rows, width)

    dp_bits, cp_bits = bits_of("dp"), bits_of("cp")
    core = ("dp", 0)
    grad_out = cotangent[0].reshape(count, width)
    grad_down = low(jnp.einsum("td,ctf->cdf", grad_out, active, preferred_element_type=jnp.float32))
    grad_down, grad_out = tie(grad_down, grad_out)
    if ndp == 2 * ncp:
        half = ff // ndp
        own = core_index == 0
        near, far = grad_down[..., :half], grad_down[..., half:]
        got = flip_bit(jnp.where(own, far, near), "dp", 0)
        down_sum = low(wide(jnp.where(own, near, far)) + wide(got))
        down_left = dp_bits[:-1] + cp_bits
        down_sum = split_bits(down_sum.reshape(ncp, ncp, -1, half), 2, down_left)
    else:
        down_sum = split_bits(grad_down.reshape(ndp, ncp, -1, ff // ndp), 2, dp_bits + cp_bits)
        down_sum, down_left = halve(down_sum, dp_bits + cp_bits, core)
    grad_active = jnp.einsum("td,cdf->ctf", grad_out, down_slabs, preferred_element_type=jnp.float32)
    grad_upper = low(grad_active * wide(slope))
    grad_upper, down_sum = tie(grad_upper, down_sum)
    grad_up = low(jnp.einsum("td,ctf->cdf", normed2, grad_upper, preferred_element_type=jnp.float32))
    grad_up, grad_upper = tie(grad_up, grad_upper)
    up_sum = split_bits(grad_up.reshape(ncp, ndp, cells, -1), 2, cp_bits + dp_bits)
    up_sum, up_left = halve(up_sum, cp_bits + dp_bits, core)
    down_state = step(begin(down_sum, down_left))
    grad_normed2 = jnp.einsum(
        "ctf,cdf->td", grad_upper, up_slabs, preferred_element_type=jnp.float32
    )
    grad_normed2, up_sum, *pieces = tie(grad_normed2, up_sum, *held(down_state))
    down_state = step(placed(down_state, pieces))
    grad_residual = wide(grad_out) + normalize_back(grad_normed2, gains[1], hat2, rstd2)
    grad_branch = low(grad_residual)
    grad_attended = low(
        jnp.einsum("td,ed->te", grad_branch, out_own, preferred_element_type=jnp.float32)
    )
    grad_attended, grad_branch, *pieces = tie(grad_attended, grad_branch, *held(down_state))
    down_state = placed(down_state, pieces)
    grad_attended = rows_to_heads(
        grad_attended.reshape(micro, rows, -1), mine, part, micro, parts, crossed
    )
    grad_proj = low(
        jnp.einsum("te,td->ed", attended, grad_branch, preferred_element_type=jnp.float32)
    )
    stride = slots * PAIR
    grad_proj = jnp.concatenate(
        [grad_proj[k * stride : k * stride + main] for k in range(parts)]
        + [grad_proj[main : main + HEAD_DIM]],
        axis=0,
    )
    proj_sum = split_bits(grad_proj.reshape(ndp, cells, width), 1, dp_bits)
    proj_sum, proj_left = halve(proj_sum, dp_bits, core)
    lead = len(proj_left)
    proj_sum = jnp.moveaxis(proj_sum.reshape(proj_sum.shape[:-1] + (ncp, -1)), -2, lead)
    proj_sum = proj_sum.reshape((2,) * (lead + len(cp_bits)) + proj_sum.shape[lead + 1 :])
    proj_left = proj_left + cp_bits

    grad_attended, layer_out, up_sum, proj_sum, *pieces = tie(
        grad_attended, layer_out, up_sum, proj_sum, *held(down_state)
    )
    down_state = step(placed(down_state, pieces))
    up_state = step(begin(up_sum, up_left))
    proj_state = step(begin(proj_sum, proj_left))
    grad_mixed = attention_backward(
        mixed,
        to_places(grad_attended),
        attended_own,
        rowat,
        tile_full,
        tile_high,
        first,
        log_sums,
        TILE,
        own_heads,
    )
    states = (down_state, up_state, proj_state)
    grad_mixed, *pieces = tie(grad_mixed, *[piece for state in states for piece in held(state)])
    down_state, up_state, proj_state = (
        placed(state, [pieces.pop(0) for _ in state]) for state in states
    )
    grad_normed1 = low(
        jnp.einsum("te,de->td", grad_mixed, mix_own, preferred_element_type=jnp.float32)
    )
    grad_normed1, grad_mixed = tie(grad_normed1, grad_mixed)
    grad_normed1 = wide(
        scatter_pack(to_devices(grad_normed1), mine, micro, crossed).reshape(count, width)
    )
    grad_mix = jnp.einsum("td,te->de", pack_low, grad_mixed, preferred_element_type=jnp.float32)
    keep, send = mix_spread(
        low(grad_mix).reshape(ndp, cells, -1), part, core_index, main, parts, ncp
    )
    mix_sum = low(wide(keep) + wide(flip_bit(send, "dp", 0)))
    mix_bits = dp_bits[:-1] + cp_bits
    mix_sum = mix_sum.reshape((2,) * len(mix_bits) + (-1, PAIR))
    grad_mix_own = finish(begin(mix_sum, mix_bits)).reshape(-1, cells, PAIR)
    grad_mix_own = jnp.stack(unpack_lanes(list(grad_mix_own), width // ncp), axis=1)
    mixed_sums = from_own_columns(kind_major(jnp.sum(wide(grad_mixed), axis=0)))
    grad_down_own = finish(down_state).T
    grad_up_own = finish(up_state)
    grad_proj_own = finish(proj_state)

    hat1, rstd1 = normalize(source)
    grad_tokens = grad_residual + normalize_back(grad_normed1, gains[0], hat1, rstd1)
    grad_tokens = low(grad_tokens).reshape(1, micro, rows, width)

    vectors = (
        jnp.stack((jnp.sum(grad_normed1 * hat1, axis=0), jnp.sum(grad_normed2 * hat2, axis=0))),
        jnp.stack((jnp.sum(grad_normed1, axis=0), jnp.sum(grad_normed2, axis=0))),
        jnp.stack((mixed_sums[0], mixed_sums[2])),
        jnp.stack((jnp.sum(wide(grad_branch), axis=0), jnp.sum(wide(grad_out), axis=0))),
    )
    flat = [item.reshape(2, ndp, cells).transpose(1, 0, 2).reshape(ndp, -1) for item in vectors]
    flat.append(jnp.sum(wide(grad_upper), axis=1).reshape(ndp, -1))
    flat = split_bits(jnp.concatenate(flat, axis=1), 1, dp_bits)
    left = dp_bits
    for bit in sorted(dp_bits):
        flat, left = halve(flat, left, bit)
    for axis, place in sorted(cp_bits):
        flat = flat + flip_bit(flat, axis, place)
    sums = flat
    parts_out = [sums[k * 2 * cells : (k + 1) * 2 * cells].reshape(2, cells) for k in range(4)]
    grad_upb = sums[8 * cells :]
    return (
        layer_out,
        grad_tokens,
        parts_out[0],
        parts_out[1],
        grad_mix_own,
        parts_out[2],
        grad_proj_own,
        grad_up_own,
        grad_upb,
        grad_down_own,
        parts_out[3],
    )


def solution(mesh):
    placed = (
        P("dp", None, "cp", None),
        P("dp", None, "cp", None),
        P("dp", None, None),
        P("dp", None, None),
        P(None, "dp"),
        P(None, "dp"),
        P("dp", None, "cp"),
        P(None, "dp"),
        P("dp", "cp"),
        P("dp", "cp"),
        P("dp"),
        P("dp", "cp"),
        P(None, "dp"),
    )
    return jax.shard_map(
        per_device,
        mesh=mesh,
        in_specs=placed,
        out_specs=(
            P("dp", None, "cp", None),
            P("dp", None, "cp", None),
            P(None, "dp"),
            P(None, "dp"),
            P("dp", None, "cp"),
            P(None, "dp"),
            P("dp", "cp"),
            P("dp", "cp"),
            P("dp"),
            P("dp", "cp"),
            P(None, "dp"),
        ),
        check_vma=False,
    )
```

time: 2640 us -> 1140 us (0.43)
  matrix products: 1060 us -> 196 us
  waiting for transfers between devices: 846 us -> 215 us
  Pallas kernels: 0 us -> 251 us
  blocking collectives: 155 us -> 14.4 us
  other arithmetic: 260 us -> 141 us
  starting transfers between devices: 1.22 us -> 94.5 us
  local copies, waits for them, and re-layouts: 276 us -> 206 us
    dot_general x66 -> x11, matrix products: 1060 us -> 196 us  [the longest x1 26.2 us: per_device(): jnp.einsum('td,cdf->ctf', grad_out, down_slabs, preferred_element_type=jn...]
    reduce_scatter x4 -> x0, waiting for transfers between devices: 448 us -> none  [the longest x2 249 us: per_device(): lax.psum_scatter(back_result[1].astype(jnp.bfloat16), 'cp', scatter_dimen...]
    pallas_call x0 -> x8, Pallas kernels: none -> 251 us  [the longest x1 99.9 us: attention_backward(): pl.pallas_call(functools.partial(backward_kernel, tile, heads), in_specs=...]
    unnamed x26 -> x4, waiting for transfers between devices: 206 us -> 1.39 us
    ppermute x0 -> x53, waiting for transfers between devices: none -> 175 us  [the longest x10 66.1 us: flip_role(): return lax.ppermute(values, ('dp', 'cp'), pairs)]
    all_gather x10 -> x4, waiting for transfers between devices: 192 us -> 38.9 us  [gather(): return lax.all_gather(shard, axes, axis=0, tiled=False)]
    ppermute x0 -> x53, starting transfers between devices: none -> 94.4 us  [the longest x41 80.9 us: flip_bit(): lax.ppermute(values, axis, [(i, i ^ 1 << place) for i in range(lax.axis_s...]
    reduce_sum x52 -> x14, other arithmetic: 127 us -> 34.2 us  [the longest x1 8.04 us: per_device(): jnp.sum(grad_normed2 * hat2, axis=0)]
  transfers between devices with their start and end apart: 20 -> 57, of which waited for: 10 -> 25; matrix products, arithmetic and copies ran while one was open for 50% -> 32% of each run, Pallas kernels for 0% -> 22%
where the time goes in v1:
time: 1140 us; the launch traced here: 1130 us
  Pallas kernels  251 us (22%)
  waiting for transfers between devices  215 us (19%)
  local copies, waits for them, and re-layouts  206 us (18%)
  matrix products  196 us (17%)
  other arithmetic  141 us (12%)
  starting transfers between devices  94.5 us (8%)
  between operations  15.5 us (1%)
  blocking collectives  14.4 us (1%)
    pallas_call x1, Pallas kernels, attention_backward(): pl.pallas_call(functools.partial(backward_kernel, tile, heads), in_specs=...  99.9 us
    ppermute x41, starting transfers between devices, flip_bit(): lax.ppermute(values, axis, [(i, i ^ 1 << place) for i in range(lax.axis_s...  80.9 us
    ppermute x10, waiting for transfers between devices, flip_role(): return lax.ppermute(values, ('dp', 'cp'), pairs)  66.1 us
    pallas_call x1, Pallas kernels, attention_forward(): pl.pallas_call(functools.partial(forward_kernel, tile, heads), in_specs=[...  63.5 us
    ppermute x41, waiting for transfers between devices, flip_bit(): lax.ppermute(values, axis, [(i, i ^ 1 << place) for i in range(lax.axis_s...  55.2 us
    pallas_call x1, Pallas kernels, up_forward(): pl.pallas_call(up_kernel, grid=(slabs, total // span), in_specs=[pl.Block...  43 us
    all_gather x4, waiting for transfers between devices, gather(): return lax.all_gather(shard, axes, axis=0, tiled=False)  38.9 us
    ppermute x1, waiting for transfers between devices, heads_to_rows(): lax.ppermute(values[3], 'cp', [(i, i ^ 3) for i in range(4)])  37.6 us
  transfers between devices with their start and end apart: 57, of which 25 were waited for; matrix products, arithmetic and copies ran while one was open for 32% of the time, Pallas kernels for 22%

profile of v1, /device:TPU:0, one launch (start us, length us, event | category | flops | bytes accessed | tf_op | source)
XLA Modules:
  0.0 1134.3 jit_solution(5079350696823194670)
XLA Ops:
  38.2 14.4 %all-gather.4 = bf16[8,1,1632]{2,1,0:T(2,128)(2,1)S(1)} all-gather(bf16[1,1,1632]{2,1,0:T(2,128)(2,1)S(1)} %bitcast.449), channel_id=1, replica_groups=mesh['dp'=8,'cp'=4] {'dp'}, dimensions={0}, use_global_device_ids=true | all-gather | bytes 29376 | tf_op jit(solution)/shard_map/all_gather | solution.py:688
  85.3 5.6 copy.228
  93.5 14.1 %collective-permute-done.2 = bf16[768,1088]{0,1:T(8,128)(2,1)S(1)} collective-permute-done((bf16[768,1088]{0,1:T(8,128)(2,1)}, bf16[768,1088]{0,1:T(8,128)(2,1)S(1)}, u32[]{:S(2)}, u32[]{:S(2)}) %collective-permute-start.2) | collective-permute-done | bytes 1671200 | tf_op jit(solution)/shard_map/ppermute | solution.py:572
  107.5 5.4 pad_maximum_fusion
  117.4 38.9 %all-gather.10.cloned.1.call-done = bf16[224,136,128]{2,1,0:T(8,128)(2,1)} async-done(((bf16[7,136,128]{2,1,0:T(8,128)(2,1)}), bf16[224,136,128]{2,1,0:T(8,128)(2,1)}) %all-gather.10.cloned.1.call-update) | async-done | bytes 7798800 | tf_op jit(solution)/shard_map/all_gather | solution.py:680
  156.4 8.8 mix_take.1
  165.1 10.3 copy.222
  175.5 10.2 norm_rows.1
  185.7 20.1 %add_convert_fusion.qkv_ref = bf16[3072,1920]{1,0:T(8,128)(2,1)} fusion(bf16[3072,1088]{1,0:T(8,128)(2,1)} %norm_rows.1, bf16[1088,1920]{1,0:T(8,128)(2,1)S(1)} %bitcast.459, f32[1920]{0:T(1024)S(1)} %copy-done.75), kind=kOutput, calls=%fused_computation.7 | convolution fusion | flops 12846366720 | bytes 22666752 | tf_op jit(solution)/shard_map/dot_general | solution.py:759
  205.8 63.5 %attention_forward.1 = (bf16[3072,640]{1,0:T(8,128)(2,1)}, f32[9,3072]{1,0:T(8,128)}) custom-call(s32[12]{0:T(128)} %fusion.74.rowat, s32[12]{0:T(128)} %and_select_fusion.3.low, s32[12]{0:T(128)} %iota_minimum_fusion.mid, bf16[3072,1920]{1,0:T(8,128)(2,1)} %add_convert_fusion.qkv_ref, s32[1,3072]{1,0:T(1,128)} %bitcast.443), custom_call_target="tpu_custom_call" | custom-call | flops 85359001600 | bytes 11796480 | tf_op jit(solution)/shard_map/attention_forward/pallas_call | solution.py:129
  271.8 21.7 %collective-permute-done.3 = bf16[768,640]{1,0:T(8,128)(2,1)S(1)} collective-permute-done((bf16[768,640]{1,0:T(8,128)(2,1)S(1)}, bf16[768,640]{1,0:T(8,128)(2,1)S(1)}, u32[]{:S(2)}, u32[]{:S(2)}) %collective-permute-start.3) | collective-permute-done | bytes 983072 | tf_op jit(solution)/shard_map/ppermute | solution.py:572
  295.8 37.6 %collective-permute-done.5 = bf16[768,640]{1,0:T(8,128)(2,1)S(1)} collective-permute-done((bf16[768,640]{1,0:T(8,128)(2,1)S(1)}, bf16[768,640]{1,0:T(8,128)(2,1)S(1)}, u32[]{:S(2)}, u32[]{:S(2)}) %collective-permute-start.5) | collective-permute-done | bytes 983072 | tf_op jit(solution)/shard_map/ppermute | solution.py:610
  333.4 16.3 %collective-permute-done.4 = bf16[768,640]{1,0:T(8,128)(2,1)S(1)} collective-permute-done((bf16[768,640]{1,0:T(8,128)(2,1)S(1)}, bf16[768,640]{1,0:T(8,128)(2,1)S(1)}, u32[]{:S(2)}, u32[]{:S(2)}) %collective-permute-start.4) | collective-permute-done | bytes 983072 | tf_op jit(solution)/shard_map/ppermute | solution.py:572
  354.2 5.7 fusion.89
  366.1 43.0 %up_forward.1 = (bf16[4,1536,1088]{2,1,0:T(8,128)(2,1)}, bf16[4,1536,1088]{2,1,0:T(8,128)(2,1)}) custom-call(bf16[1536,1088]{1,0:T(8,128)(2,1)} %add_convert_fusion.3.x_ref, bf16[4,1088,1088]{2,1,0:T(8,128)(2,1)} %bitcast.454, f32[4,1,1088]{2,1,0:T(1,128)} %reshape_reshape.12.b_ref), custom_call_target="tpu_custom_call" | custom-call | flops 34604998656 | bytes 12812288 | tf_op jit(solution)/shard_map/up_forward/pallas_call | solution.py:287
  409.1 21.4 %fusion.2 = bf16[4,1088,1088]{1,2,0:T(8,128)(2,1)S(1)} fusion(bf16[4,1536,1088]{2,1,0:T(8,128)(2,1)} %get-tuple-element.51, bf16[1536,1088,1]{1,0,2:T(8,128)(2,1)} %bitcast.417), kind=kOutput, calls=%fused_computation.8 | convolution fusion | flops 14550581248 | bytes 26181632 | tf_op jit(solution)/shard_map/td,ctf->cdf/dot_general | solution.py:790
  438.9 14.2 %merge_lanes.3 = bf16[4,1088,1088]{2,1,0:T(8,128)(2,1)} custom-call(bf16[4,2,1088,544]{3,2,1,0:T(8,128)(2,1)} %bitcast.453), custom_call_target="tpu_custom_call" | custom-call | flops 9228000256 | bytes 9469952 | tf_op jit(solution)/shard_map/merge_lanes/pallas_call | solution.py:338
  453.1 26.2 %fusion.1 = bf16[4,1536,1088]{2,1,0:T(8,128)(2,1)} fusion(bf16[4,1536,1088]{2,1,0:T(8,128)(2,1)} %get-tuple-element.53, bf16[4,1088,1088]{2,1,0:T(8,128)(2,1)} %merge_lanes.3, bf16[1536,1088]{1,0:T(8,128)(2,1)S(1)} %bitcast.418), kind=kOutput, calls=%fused_computation.3 | convolution fusion | flops 14565900288 | bytes 39550976 | tf_op jit(solution)/shard_map/td,cdf->ctf/dot_general | solution.py:803
  479.3 9.4 add_convert_fusion.1
  488.7 8.6 copy.233
  497.2 23.2 %fusion.3 = bf16[4,1088,1088]{1,2,0:T(8,128)(2,1)} fusion(bf16[4,1536,1088]{2,1,0:T(8,128)(2,1)} %fusion.1, bf16[1536,1088]{1,0:T(8,128)(2,1)S(1)} %copy-done.32), kind=kOutput, calls=%fused_computation.9 | convolution fusion | flops 14550581248 | bytes 26181632 | tf_op jit(solution)/shard_map/td,ctf->cdf/dot_general | solution.py:806
  520.4 14.5 %copy.236 = bf16[4,1088,1088]{2,1,0:T(8,128)(2,1)} copy(bf16[4,1088,1088]{1,2,0:T(8,128)(2,1)} %fusion.3) | data formatting | bytes 18939904 | tf_op jit(solution)/shard_map/optimization_barrier | solution.py:532
  534.9 5.0 dynamic-slice_bitcast_fusion
  540.4 25.5 %fusion.8 = bf16[1536,1088]{1,0:T(8,128)(2,1)} fusion(f32[1536,1088]{1,0:T(8,128)} %copy-done.5, bf16[4,1536,1088]{2,1,0:T(8,128)(2,1)} %get-tuple-element.51, bf16[4,1088,1088]{2,1,0:T(8,128)(2,1)} %merge_lanes.3, f32[1088]{0:T(1024)S(1)} %copy-done.73), kind=kOutput, calls=%fused_computation.24 | convolution fusion | flops 14550859776 | bytes 32870656 | tf_op jit(solution)/shard_map/ctf,cdf->td/dot_general | solution.py:782
  573.7 23.6 %convolution_bitcast_fusion.2 = f32[1536,1088]{0,1:T(8,128)} fusion(bf16[4,1536,1088]{2,1,0:T(8,128)(2,1)} %fusion.1, bf16[4,1088,1088]{2,1,0:T(8,128)(2,1)} %bitcast.455), kind=kOutput, calls=%fused_computation.21 | convolution fusion | flops 14545846272 | bytes 29523968 | tf_op jit(solution)/shard_map/ctf,cdf->td/dot_general | solution.py:811
  597.3 6.6 collective-permute-done.9
  607.0 5.8 fusion.4
  612.8 7.8 copy.238
  620.7 8.0 multiply_reduce_fusion
  633.4 5.6 fusion.79
  639.0 8.7 convolution_convert_fusion.3
  650.5 4.8 convolution_convert_fusion.5
  670.0 7.6 convert_reduce_fusion
  688.6 15.9 %collective-permute-done.14 = bf16[768,640]{1,0:T(8,128)(2,1)} collective-permute-done((bf16[768,640]{1,0:T(8,128)(2,1)}, bf16[768,640]{1,0:T(8,128)(2,1)}, u32[]{:S(2)}, u32[]{:S(2)}) %collective-permute-start.14) | collective-permute-done | bytes 983072 | tf_op jit(solution)/shard_map/ppermute | solution.py:639
  720.5 5.8 copy.255
  738.3 99.9 %attention_backward.1 = bf16[3072,1920]{1,0:T(8,128)(2,1)} custom-call(s32[12]{0:T(128)} %fusion.74.rowat, s32[12]{0:T(128)} %get-tuple-element.179.full, s32[12]{0:T(128)} %get-tuple-element.180.high, bf16[3072,1920]{1,0:T(8,128)(2,1)} %add_convert_fusion.qkv_ref, bf16[3072,640]{1,0:T(8,128)(2,1)} %bitcast.431, bf16[3072,640]{1,0:T(8,128)(2,1)} %get-tuple-element.50.o_ref, ...), custom_call_target="tpu_custom_call" | custom-call | flops 133805998080 | bytes 11796480 | tf_op jit(solution)/shard_map/attention_backward/pallas_call | solution.py:244
  847.4 8.8 collective-permute-done.18
  857.5 20.6 %convolution_convert_fusion.2 = bf16[3072,1088]{1,0:T(8,128)(2,1)} fusion(bf16[3072,1920]{1,0:T(8,128)(2,1)S(1)} %copy-done.16, bf16[1088,1920]{1,0:T(8,128)(2,1)} %bitcast.458), kind=kOutput, calls=%fused_computation.10 | convolution fusion | flops 12837912576 | bytes 22659072 | tf_op jit(solution)/shard_map/te,de->td/dot_general | solution.py:866
  878.1 16.6 %convolution_convert_fusion.4 = bf16[1088,1920]{1,0:T(8,128)(2,1)} fusion(bf16[3072,1088]{1,0:T(8,128)(2,1)S(1)} %bitcast.462, bf16[3072,1920]{1,0:T(8,128)(2,1)S(1)} %copy-done.16), kind=kOutput, calls=%fused_computation.25 | convolution fusion | flops 12836659200 | bytes 22659072 | tf_op jit(solution)/shard_map/td,te->de/dot_general | solution.py:872
  894.7 6.0 convert_reduce_fusion.1
  902.1 34.0 %collective-permute-start.52 = (bf16[136,544]{1,0:T(8,128)(2,1)}, bf16[136,544]{1,0:T(8,128)(2,1)}, u32[]{:S(2)}, u32[]{:S(2)}) collective-permute-start(bf16[136,544]{1,0:T(8,128)(2,1)} %dynamic-slice_bitcast_fusion.22), channel_id=1, source_target_pairs={{0,16},{4,20},{8,24},{12,28},{16,0},{20,4},{24,8},{28,12},{1,17},{... | collective-permute-start | bytes 443912 | tf_op jit(solution)/shard_map/ppermute | solution.py:510
  946.7 7.3 mix_spread.1
  999.3 5.8 collective-permute-done.46
  1011.6 14.1 %collective-permute-done.24 = bf16[768,1088]{0,1:T(8,128)(2,1)S(1)} collective-permute-done((bf16[768,1088]{0,1:T(8,128)(2,1)}, bf16[768,1088]{0,1:T(8,128)(2,1)S(1)}, u32[]{:S(2)}, u32[]{:S(2)}) %collective-permute-start.24) | collective-permute-done | bytes 1671200 | tf_op jit(solution)/shard_map/ppermute | solution.py:572
  1075.4 4.9 fusion.14
  1080.3 5.8 copy.256
  1087.6 6.6 collective-permute-done.35
  1110.3 4.9 collective-permute-done.37
  (547 shorter events, 319.9 us)
Async XLA Ops:
  7.2 105.7 %all-gather.12.cloned.1.call-start = ((), (), s32[]{:S(2)}) async-start(), calls=%async_computation.1 | async-start | bytes 3446784 | tf_op jit(solution)/shard_map/all_gather | solution.py:680
  7.9 148.4 %all-gather.10.cloned.1.call-start = ((), (), s32[]{:S(2)}) async-start(), calls=%async_computation | async-start | bytes 8042496 | tf_op jit(solution)/shard_map/all_gather | solution.py:680
  10.0 356.0 %all-gather.14.cloned.1.call-start = ((), (), s32[]{:S(2)}) async-start(), calls=%async_computation.2 | async-start | bytes 10340352 | tf_op jit(solution)/shard_map/all_gather | solution.py:680
  10.8 428.1 %all-gather.16.cloned.1.call-start = ((), (), s32[]{:S(2)}) async-start(), calls=%async_computation.3 | async-start | bytes 11489280 | tf_op jit(solution)/shard_map/all_gather | solution.py:680
  21.4 62.6 %collective-permute-start.1 = (bf16[768,1088]{0,1:T(8,128)(2,1)}, bf16[768,1088]{0,1:T(8,128)(2,1)}, u32[]{:S(2)}, u32[]{:S(2)}) collective-permute-start(bf16[768,1088]{0,1:T(8,128)(2,1)} %bitcast.434), channel_id=1, source_target_pairs={{0,2},{1,3},{2,0},{3,1},{4,5},{5,4},{6,7},{7,6},{8,10},{9,11},{10,... | collective-permute-start | bytes 5013512 | tf_op jit(solution)/shard_map/ppermute | solution.py:572
  28.2 65.3 %collective-permute-start = (bf16[768,1088]{0,1:T(8,128)(2,1)}, bf16[768,1088]{0,1:T(8,128)(2,1)}, u32[]{:S(2)}, u32[]{:S(2)}) collective-permute-start(bf16[768,1088]{0,1:T(8,128)(2,1)} %bitcast.424), channel_id=1, source_target_pairs={{0,1},{1,0},{2,3},{3,2},{4,6},{5,7},{6,4},{7,5},{8,9},{9,8},{10,11... | collective-permute-start | bytes 5013512 | tf_op jit(solution)/shard_map/ppermute | solution.py:572
  84.0 23.5 %collective-permute-start.2 = (bf16[768,1088]{0,1:T(8,128)(2,1)}, bf16[768,1088]{0,1:T(8,128)(2,1)S(1)}, u32[]{:S(2)}, u32[]{:S(2)}) collective-permute-start(bf16[768,1088]{0,1:T(8,128)(2,1)} %collective-permute-done.1), channel_id=1, source_target_pairs={{0,1},{1,0},{2,3},{3,2},{4,6},{5,7},{6,4},{7,5},{8,9},{9,8},{10,11... | collective-permute-start | bytes 5013512 | tf_op jit(solution)/shard_map/ppermute | solution.py:572
  270.7 22.7 %collective-permute-start.3 = (bf16[768,640]{1,0:T(8,128)(2,1)S(1)}, bf16[768,640]{1,0:T(8,128)(2,1)S(1)}, u32[]{:S(2)}, u32[]{:S(2)}) collective-permute-start(bf16[768,640]{1,0:T(8,128)(2,1)S(1)} %slice.332), channel_id=1, source_target_pairs={{0,1},{1,0},{2,3},{3,2},{4,6},{5,7},{6,4},{7,5},{8,9},{9,8},{10,11... | collective-permute-start | bytes 2949128 | tf_op jit(solution)/shard_map/ppermute | solution.py:572
  293.8 39.7 %collective-permute-start.5 = (bf16[768,640]{1,0:T(8,128)(2,1)S(1)}, bf16[768,640]{1,0:T(8,128)(2,1)S(1)}, u32[]{:S(2)}, u32[]{:S(2)}) collective-permute-start(bf16[768,640]{1,0:T(8,128)(2,1)S(1)} %get-tuple-element.193), channel_id=1, source_target_pairs={{0,3},{1,2},{2,1},{3,0},{4,7},{5,6},{6,5},{7,4},{8,11},{9,10},{10,... | collective-permute-start | bytes 2949128 | tf_op jit(solution)/shard_map/ppermute | solution.py:610
  295.3 54.4 %collective-permute-start.4 = (bf16[768,640]{1,0:T(8,128)(2,1)S(1)}, bf16[768,640]{1,0:T(8,128)(2,1)S(1)}, u32[]{:S(2)}, u32[]{:S(2)}) collective-permute-start(bf16[768,640]{1,0:T(8,128)(2,1)S(1)} %get-tuple-element.194), channel_id=1, source_target_pairs={{0,2},{1,3},{2,0},{3,1},{4,5},{5,4},{6,7},{7,6},{8,10},{9,11},{10,... | collective-permute-start | bytes 2949128 | tf_op jit(solution)/shard_map/ppermute | solution.py:572
  435.9 43.4 %collective-permute-start.6 = (bf16[4,1088,544]{1,2,0:T(8,128)(2,1)}, bf16[4,1088,544]{1,2,0:T(8,128)(2,1)}, u32[]{:S(2)}, u32[]{:S(2)}) collective-permute-start(bf16[4,1088,544]{1,2,0:T(8,128)(2,1)} %broadcast_select_fusion), channel_id=1, source_target_pairs={{0,4},{4,0},{8,12},{12,8},{16,20},{20,16},{24,28},{28,24},{1,5},{5... | collective-permute-start | bytes 14204936 | tf_op jit(solution)/shard_map/ppermute | solution.py:510
  539.9 67.0 %collective-permute-start.7 = (bf16[2,2,2,2,136,1088]{5,4,3,2,1,0:T(8,128)(2,1)}, bf16[2,2,2,2,136,1088]{5,4,3,2,1,0:T(8,128)(2,1)}, u32[]{:S(2)}, u32[]{:S(2)}) collective-permute-start(bf16[2,2,2,2,136,1088]{5,4,3,2,1,0:T(8,128)(2,1)} %dynamic-slice_bitcast_fusion), channel_id=1, source_target_pairs={{0,4},{4,0},{8,12},{12,8},{16,20},{20,16},{24,28},{28,24},{1,5},{5... | collective-permute-start | bytes 14204936 | tf_op jit(solution)/shard_map/ppermute | solution.py:510
  571.4 32.6 %collective-permute-start.9 = (bf16[2,2,2,136,544]{4,3,2,1,0:T(8,128)(2,1)S(1)}, bf16[2,2,2,136,544]{4,3,2,1,0:T(8,128)(2,1)S(1)}, u32[]{:S(2)}, u32[]{:S(2)}) collective-permute-start(bf16[2,2,2,136,544]{4,3,2,1,0:T(8,128)(2,1)S(1)} %dynamic-slice_bitcast_fusion.1), channel_id=1, source_target_pairs={{0,2},{1,3},{2,0},{3,1},{4,6},{5,7},{6,4},{7,5},{8,10},{9,11},{10,... | collective-permute-start | bytes 3551240 | tf_op jit(solution)/shard_map/ppermute | solution.py:510
  572.3 33.1 %collective-permute-start.8 = (bf16[2,2,2,136,544]{4,3,0,1,2:T(8,128)(2,1)S(1)}, bf16[2,2,2,136,544]{4,3,0,1,2:T(8,128)(2,1)S(1)}, u32[]{:S(2)}, u32[]{:S(2)}) collective-permute-start(bf16[2,2,2,136,544]{4,3,0,1,2:T(8,128)(2,1)S(1)} %dynamic-slice_bitcast_fusion.2), channel_id=1, source_target_pairs={{0,1},{1,0},{2,3},{3,2},{4,5},{5,4},{6,7},{7,6},{8,9},{9,8},{10,11... | collective-permute-start | bytes 3551240 | tf_op jit(solution)/shard_map/ppermute | solution.py:510
  631.4 17.0 %collective-permute-start.11 = (bf16[2,2,136,544]{3,2,1,0:T(8,128)(2,1)S(1)}, bf16[2,2,136,544]{3,2,1,0:T(8,128)(2,1)S(1)}, u32[]{:S(2)}, u32[]{:S(2)}) collective-permute-start(bf16[2,2,136,544]{3,2,1,0:T(8,128)(2,1)S(1)} %dynamic-slice_bitcast_fusion.6), channel_id=1, source_target_pairs={{0,1},{1,0},{2,3},{3,2},{4,5},{5,4},{6,7},{7,6},{8,9},{9,8},{10,11... | collective-permute-start | bytes 1775624 | tf_op jit(solution)/shard_map/ppermute | solution.py:510
  631.8 17.6 %collective-permute-start.10 = (bf16[2,2,136,544]{3,2,0,1:T(8,128)(2,1)S(1)}, bf16[2,2,136,544]{3,2,0,1:T(8,128)(2,1)S(1)}, u32[]{:S(2)}, u32[]{:S(2)}) collective-permute-start(bf16[2,2,136,544]{3,2,0,1:T(8,128)(2,1)S(1)} %dynamic-slice_bitcast_fusion.7), channel_id=1, source_target_pairs={{0,2},{1,3},{2,0},{3,1},{4,6},{5,7},{6,4},{7,5},{8,10},{9,11},{10,... | collective-permute-start | bytes 1775624 | tf_op jit(solution)/shard_map/ppermute | solution.py:510
  662.5 26.1 %collective-permute-start.12 = (bf16[768,640]{1,0:T(8,128)(2,1)}, bf16[768,640]{1,0:T(8,128)(2,1)}, u32[]{:S(2)}, u32[]{:S(2)}) collective-permute-start(bf16[768,640]{1,0:T(8,128)(2,1)} %get-tuple-element.203), channel_id=1, source_target_pairs={{0,1},{1,0},{2,3},{3,2},{4,6},{5,7},{6,4},{7,5},{8,9},{9,8},{10,11... | collective-permute-start | bytes 2949128 | tf_op jit(solution)/shard_map/ppermute | solution.py:572
  665.7 42.7 %collective-permute-start.15 = (bf16[2,2,136,1088]{3,2,1,0:T(8,128)(2,1)}, bf16[2,2,136,1088]{3,2,1,0:T(8,128)(2,1)}, u32[]{:S(2)}, u32[]{:S(2)}) collective-permute-start(bf16[2,2,136,1088]{3,2,1,0:T(8,128)(2,1)} %dynamic-slice_bitcast_fusion.4), channel_id=1, source_target_pairs={{0,4},{4,0},{8,12},{12,8},{16,20},{20,16},{24,28},{28,24},{1,5},{5... | collective-permute-start | bytes 3551240 | tf_op jit(solution)/shard_map/ppermute | solution.py:510
  667.2 21.4 %collective-permute-start.13 = (bf16[768,640]{1,0:T(8,128)(2,1)}, bf16[768,640]{1,0:T(8,128)(2,1)}, u32[]{:S(2)}, u32[]{:S(2)}) collective-permute-start(bf16[768,640]{1,0:T(8,128)(2,1)} %get-tuple-element.204), channel_id=1, source_target_pairs={{0,2},{1,3},{2,0},{3,1},{4,5},{5,4},{6,7},{7,6},{8,10},{9,11},{10,... | collective-permute-start | bytes 2949128 | tf_op jit(solution)/shard_map/ppermute | solution.py:572
  668.4 36.2 %collective-permute-start.14 = (bf16[768,640]{1,0:T(8,128)(2,1)}, bf16[768,640]{1,0:T(8,128)(2,1)}, u32[]{:S(2)}, u32[]{:S(2)}) collective-permute-start(bf16[768,640]{1,0:T(8,128)(2,1)} %get-tuple-element.205), channel_id=1, source_target_pairs={{0,3},{1,2},{2,1},{3,0},{4,7},{5,6},{6,5},{7,4},{8,11},{9,10},{10,... | collective-permute-start | bytes 2949128 | tf_op jit(solution)/shard_map/ppermute | solution.py:639
  729.9 111.2 %collective-permute-start.17 = (bf16[2,136,544]{2,1,0:T(8,128)(2,1)}, bf16[2,136,544]{2,1,0:T(8,128)(2,1)}, u32[]{:S(2)}, u32[]{:S(2)}) collective-permute-start(bf16[2,136,544]{2,1,0:T(8,128)(2,1)} %dynamic-slice_bitcast_fusion.14), channel_id=1, source_target_pairs={{0,8},{4,12},{8,0},{12,4},{16,24},{20,28},{24,16},{28,20},{1,9},{5... | collective-permute-start | bytes 887816 | tf_op jit(solution)/shard_map/ppermute | solution.py:510
  731.4 111.2 %collective-permute-start.16 = (bf16[2,136,544]{2,1,0:T(8,128)(2,1)}, bf16[2,136,544]{2,1,0:T(8,128)(2,1)}, u32[]{:S(2)}, u32[]{:S(2)}) collective-permute-start(bf16[2,136,544]{2,1,0:T(8,128)(2,1)} %dynamic-slice_bitcast_fusion.15), channel_id=1, source_target_pairs={{0,8},{4,12},{8,0},{12,4},{16,24},{20,28},{24,16},{28,20},{1,9},{5... | collective-permute-start | bytes 887816 | tf_op jit(solution)/shard_map/ppermute | solution.py:510
  732.7 105.5 %collective-permute-start.21 = (bf16[2,2,2,64,272]{4,3,0,1,2:T(8,128)(2,1)}, bf16[2,2,2,64,272]{4,3,0,1,2:T(8,128)(2,1)}, u32[]{:S(2)}, u32[]{:S(2)}) collective-permute-start(bf16[2,2,2,64,272]{4,3,0,1,2:T(8,128)(2,1)} %dynamic-slice_bitcast_fusion.13), channel_id=1, source_target_pairs={{0,2},{1,3},{2,0},{3,1},{4,6},{5,7},{6,4},{7,5},{8,10},{9,11},{10,... | collective-permute-start | bytes 835592 | tf_op jit(solution)/shard_map/ppermute | solution.py:510
  735.8 108.5 %collective-permute-start.20 = (bf16[2,2,2,72,272]{4,3,0,1,2:T(8,128)(2,1)}, bf16[2,2,2,72,272]{4,3,0,1,2:T(8,128)(2,1)}, u32[]{:S(2)}, u32[]{:S(2)}) collective-permute-start(bf16[2,2,2,72,272]{4,3,0,1,2:T(8,128)(2,1)} %dynamic-slice_bitcast_fusion.12), channel_id=1, source_target_pairs={{0,1},{1,0},{2,3},{3,2},{4,5},{5,4},{6,7},{7,6},{8,9},{9,8},{10,11... | collective-permute-start | bytes 940040 | tf_op jit(solution)/shard_map/ppermute | solution.py:510
  737.0 108.5 %collective-permute-start.19 = (bf16[2,2,2,64,1088]{4,3,2,1,0:T(8,128)(2,1)}, bf16[2,2,2,64,1088]{4,3,2,1,0:T(8,128)(2,1)}, u32[]{:S(2)}, u32[]{:S(2)}) collective-permute-start(bf16[2,2,2,64,1088]{4,3,2,1,0:T(8,128)(2,1)} %dynamic-slice_bitcast_fusion.5), channel_id=1, source_target_pairs={{0,2},{1,3},{2,0},{3,1},{4,6},{5,7},{6,4},{7,5},{8,10},{9,11},{10,... | collective-permute-start | bytes 3342344 | tf_op jit(solution)/shard_map/ppermute | solution.py:510
  838.3 17.8 %collective-permute-start.18 = (bf16[2,2,2,72,1088]{4,3,2,1,0:T(8,128)(2,1)S(1)}, bf16[2,2,2,72,1088]{4,3,2,1,0:T(8,128)(2,1)S(1)}, u32[]{:S(2)}, u32[]{:S(2)}) collective-permute-start(bf16[2,2,2,72,1088]{4,3,2,1,0:T(8,128)(2,1)S(1)} %dynamic-slice_bitcast_fusion.3), channel_id=1, source_target_pairs={{0,1},{1,0},{2,3},{3,2},{4,5},{5,4},{6,7},{7,6},{8,9},{9,8},{10,11... | collective-permute-start | bytes 3760136 | tf_op jit(solution)/shard_map/ppermute | solution.py:510
  902.1 55.2 %collective-permute-start.52 = (bf16[136,544]{1,0:T(8,128)(2,1)}, bf16[136,544]{1,0:T(8,128)(2,1)}, u32[]{:S(2)}, u32[]{:S(2)}) collective-permute-start(bf16[136,544]{1,0:T(8,128)(2,1)} %dynamic-slice_bitcast_fusion.22), channel_id=1, source_target_pairs={{0,16},{4,20},{8,24},{12,28},{16,0},{20,4},{24,8},{28,12},{1,17},{... | collective-permute-start | bytes 443912 | tf_op jit(solution)/shard_map/ppermute | solution.py:510
  936.1 22.7 %collective-permute-start.51 = (bf16[136,544]{1,0:T(8,128)(2,1)}, bf16[136,544]{1,0:T(8,128)(2,1)}, u32[]{:S(2)}, u32[]{:S(2)}) collective-permute-start(bf16[136,544]{1,0:T(8,128)(2,1)} %dynamic-slice_bitcast_fusion.23), channel_id=1, source_target_pairs={{0,16},{4,20},{8,24},{12,28},{16,0},{20,4},{24,8},{28,12},{1,17},{... | collective-permute-start | bytes 443912 | tf_op jit(solution)/shard_map/ppermute | solution.py:510
  936.8 17.3 %collective-permute-start.42 = (bf16[2,2,64,272]{3,2,0,1:T(8,128)(2,1)}, bf16[2,2,64,272]{3,2,0,1:T(8,128)(2,1)}, u32[]{:S(2)}, u32[]{:S(2)}) collective-permute-start(bf16[2,2,64,272]{3,2,0,1:T(8,128)(2,1)} %dynamic-slice_bitcast_fusion.21), channel_id=1, source_target_pairs={{0,1},{1,0},{2,3},{3,2},{4,5},{5,4},{6,7},{7,6},{8,9},{9,8},{10,11... | collective-permute-start | bytes 417800 | tf_op jit(solution)/shard_map/ppermute | solution.py:510
  938.1 24.2 %collective-permute-start.39 = (bf16[2,2,72,272]{3,2,0,1:T(8,128)(2,1)}, bf16[2,2,72,272]{3,2,0,1:T(8,128)(2,1)}, u32[]{:S(2)}, u32[]{:S(2)}) collective-permute-start(bf16[2,2,72,272]{3,2,0,1:T(8,128)(2,1)} %dynamic-slice_bitcast_fusion.20), channel_id=1, source_target_pairs={{0,2},{1,3},{2,0},{3,1},{4,6},{5,7},{6,4},{7,5},{8,10},{9,11},{10,... | collective-permute-start | bytes 470024 | tf_op jit(solution)/shard_map/ppermute | solution.py:510
  938.9 44.1 %collective-permute-start.48 = (bf16[2,2,64,1088]{3,2,1,0:T(8,128)(2,1)}, bf16[2,2,64,1088]{3,2,1,0:T(8,128)(2,1)}, u32[]{:S(2)}, u32[]{:S(2)}) collective-permute-start(bf16[2,2,64,1088]{3,2,1,0:T(8,128)(2,1)} %dynamic-slice_bitcast_fusion.9), channel_id=1, source_target_pairs={{0,1},{1,0},{2,3},{3,2},{4,5},{5,4},{6,7},{7,6},{8,9},{9,8},{10,11... | collective-permute-start | bytes 1671176 | tf_op jit(solution)/shard_map/ppermute | solution.py:510
  954.1 31.1 %collective-permute-start.45 = (bf16[2,2,72,1088]{3,2,1,0:T(8,128)(2,1)S(1)}, bf16[2,2,72,1088]{3,2,1,0:T(8,128)(2,1)S(1)}, u32[]{:S(2)}, u32[]{:S(2)}) collective-permute-start(bf16[2,2,72,1088]{3,2,1,0:T(8,128)(2,1)S(1)} %dynamic-slice_bitcast_fusion.8), channel_id=1, source_target_pairs={{0,2},{1,3},{2,0},{3,1},{4,6},{5,7},{6,4},{7,5},{8,10},{9,11},{10,... | collective-permute-start | bytes 1880072 | tf_op jit(solution)/shard_map/ppermute | solution.py:510
  957.3 30.9 %collective-permute-start.23 = (bf16[768,1088]{0,1:T(8,128)(2,1)S(1)}, bf16[768,1088]{0,1:T(8,128)(2,1)}, u32[]{:S(2)}, u32[]{:S(2)}) collective-permute-start(bf16[768,1088]{0,1:T(8,128)(2,1)S(1)} %copy.246), channel_id=1, source_target_pairs={{0,1},{1,0},{2,3},{3,2},{4,6},{5,7},{6,4},{7,5},{8,9},{9,8},{10,11... | collective-permute-start | bytes 5013512 | tf_op jit(solution)/shard_map/ppermute | solution.py:572
  958.8 49.0 %collective-permute-start.22 = (bf16[768,1088]{0,1:T(8,128)(2,1)}, bf16[768,1088]{0,1:T(8,128)(2,1)}, u32[]{:S(2)}, u32[]{:S(2)}) collective-permute-start(bf16[768,1088]{0,1:T(8,128)(2,1)} %copy.244), channel_id=1, source_target_pairs={{0,1},{1,0},{2,3},{3,2},{4,6},{5,7},{6,4},{7,5},{8,9},{9,8},{10,11... | collective-permute-start | bytes 5013512 | tf_op jit(solution)/shard_map/ppermute | solution.py:572
  982.3 82.5 %collective-permute-start.30 = (bf16[4,4,7,136,128]{4,3,2,1,0:T(8,128)(2,1)}, bf16[4,4,7,136,128]{4,3,2,1,0:T(8,128)(2,1)}, u32[]{:S(2)}, u32[]{:S(2)}) collective-permute-start(bf16[4,4,7,136,128]{4,3,2,1,0:T(8,128)(2,1)} %get-tuple-element.78), channel_id=1, source_target_pairs={{0,4},{4,0},{8,12},{12,8},{16,20},{20,16},{24,28},{28,24},{1,5},{5... | collective-permute-start | bytes 11698184 | tf_op jit(solution)/shard_map/ppermute | solution.py:510
  985.1 10.1 collective-permute-start.49
  986.3 18.8 %collective-permute-start.46 = (bf16[2,72,1088]{2,1,0:T(8,128)(2,1)}, bf16[2,72,1088]{2,1,0:T(8,128)(2,1)}, u32[]{:S(2)}, u32[]{:S(2)}) collective-permute-start(bf16[2,72,1088]{2,1,0:T(8,128)(2,1)} %dynamic-slice_bitcast_fusion.16), channel_id=1, source_target_pairs={{0,8},{4,12},{8,0},{12,4},{16,24},{20,28},{24,16},{28,20},{1,9},{5... | collective-permute-start | bytes 940040 | tf_op jit(solution)/shard_map/ppermute | solution.py:510
  995.1 30.6 %collective-permute-start.24 = (bf16[768,1088]{0,1:T(8,128)(2,1)}, bf16[768,1088]{0,1:T(8,128)(2,1)S(1)}, u32[]{:S(2)}, u32[]{:S(2)}) collective-permute-start(bf16[768,1088]{0,1:T(8,128)(2,1)} %copy.248), channel_id=1, source_target_pairs={{0,2},{1,3},{2,0},{3,1},{4,5},{5,4},{6,7},{7,6},{8,10},{9,11},{10,... | collective-permute-start | bytes 5013512 | tf_op jit(solution)/shard_map/ppermute | solution.py:572
  996.3 10.8 collective-permute-start.50
  1007.0 39.8 %collective-permute-start.47 = (bf16[72,1088]{1,0:T(8,128)(2,1)}, bf16[72,1088]{1,0:T(8,128)(2,1)}, u32[]{:S(2)}, u32[]{:S(2)}) collective-permute-start(bf16[72,1088]{1,0:T(8,128)(2,1)} %dynamic-slice_bitcast_fusion.24), channel_id=1, source_target_pairs={{0,16},{4,20},{8,24},{12,28},{16,0},{20,4},{24,8},{28,12},{1,17},{... | collective-permute-start | bytes 470024 | tf_op jit(solution)/shard_map/ppermute | solution.py:510
  1062.9 23.3 %collective-permute-start.29 = (f32[1632]{0:T(1024)}, f32[1632]{0:T(1024)}, u32[]{:S(2)}, u32[]{:S(2)}) collective-permute-start(f32[1632]{0:T(1024)} %add.456), channel_id=1, source_target_pairs={{0,2},{1,3},{2,0},{3,1},{4,6},{5,7},{6,4},{7,5},{8,10},{9,11},{10,... | collective-permute-start | bytes 19592 | tf_op jit(solution)/shard_map/ppermute | solution.py:510
  1072.8 21.4 %collective-permute-start.35 = (bf16[2,2,2,472,128]{4,3,0,1,2:T(8,128)(2,1)}, bf16[2,2,2,472,128]{4,3,0,1,2:T(8,128)(2,1)}, u32[]{:S(2)}, u32[]{:S(2)}) collective-permute-start(bf16[2,2,2,472,128]{4,3,0,1,2:T(8,128)(2,1)} %bitcast.395), channel_id=1, source_target_pairs={{0,2},{1,3},{2,0},{3,1},{4,6},{5,7},{6,4},{7,5},{8,10},{9,11},{10,... | collective-permute-start | bytes 2899976 | tf_op jit(solution)/shard_map/ppermute | solution.py:510
  1073.9 23.2 %collective-permute-start.31 = (bf16[2,2,2,480,128]{4,3,0,1,2:T(8,128)(2,1)}, bf16[2,2,2,480,128]{4,3,0,1,2:T(8,128)(2,1)}, u32[]{:S(2)}, u32[]{:S(2)}) collective-permute-start(bf16[2,2,2,480,128]{4,3,0,1,2:T(8,128)(2,1)} %bitcast.394), channel_id=1, source_target_pairs={{0,1},{1,0},{2,3},{3,2},{4,5},{5,4},{6,7},{7,6},{8,9},{9,8},{10,11... | collective-permute-start | bytes 2949128 | tf_op jit(solution)/shard_map/ppermute | solution.py:510
  1095.7 10.3 collective-permute-start.36
  1098.5 9.8 collective-permute-start.32
  1107.2 8.0 collective-permute-start.37
  1108.5 10.6 collective-permute-start.33
  1115.3 7.5 collective-permute-start.38
  (102 other events, 1507.9 us)
Sparse Core Ops, SparseCore 0:
  10.9 66.9 all-gather.11
  81.3 75.0 all-gather.9
  159.2 83.0 all-gather.13
  245.0 120.6 all-gather.15
